TPU v7x, 32 devices: a whole 2x2x4 slice. The times are simulated.
32 devices in a mesh: groups: 2 (over y), seq: 4 (over z), dp: 2 (over x), strand: 2 (over core).
Axes of the slice: x: 2, y: 2, z: 4, core: 2. Of those that a mesh axis runs over, the one named last changes fastest.
Arguments:
- tokens: int32 [4, 2048], P(('groups', 'dp'), 'seq'), parts along dimension 0, may hold values from 0 to 3
- stem_table: bfloat16 [15, 4, 1536], replicated, may hold values from -1.5 to 1.5
- conv_weight: bfloat16 [3, 1536, 768], P(None, 'dp'), may hold values from -0.09375 to 0.09375
- gain_in: float32 [1536], replicated, may hold values from 0.1 to 1.9
- gain_mid: float32 [768], replicated, may hold values from 0.1 to 1.9
- point_weight: bfloat16 [768, 1536], P('dp'), may hold values from -0.21875 to 0.21875
Outputs:
- embedding: bfloat16 [4, 2048, 1536], P(('groups', 'dp'), 'seq', 'strand'), parts along dimension 0
There are 2 independent parts, one for each index of `groups`. A program takes and returns all parts, laid end to end along the dimension named above; an argument that names none is the same for every part. Nothing has to cross between parts.
All inputs are finite; a program needn't handle non-finite values.
Results may differ from a plain program's by a relative error of at most 0.009.
Values may be sent and summed in bfloat16 or wider, within the bound.
No kernel may reach another device: no remote copies, remote signals or barrier semaphores. Data moves between devices by JAX's collectives and lax.ppermute only.
A program may use at most 64 MiB of HBM per device.

v0:
```python
import functools

import jax
import jax.numpy as jnp
from jax import lax
from jax.experimental import pallas as pl
from jax.experimental.pallas import tpu as pltpu
from jax.sharding import PartitionSpec as P

DILATION = 256
EPS = 1e-06
ROW_STEP = 128
CHUNKS = ((0, 96), (96, 96), (192, 64))
TAILS = ((0, 1), (2,))
EARLY_TAPS, LATE_TAPS = (0, 1), (2,)
KINDS = 4
TABLE = 16 * KINDS
FLOPS = {
    "early": 0.1,
    "load": 0.1,
    "sent0": 15.0,
    "sent1": 0.5,
    "sent2": 15.0,
    "own": 15.0,
    "middle0": 0.05,
    "middle1": 5.0,
    "final0": 0.5,
    "final1": 15.0,
}
MIB = 2**20


def pair_pairs(axis, first):
    count = lax.axis_size(axis)
    pairs = [(i, i + 1) for i in range(first, count - 1, 2)]
    return pairs + [(target, source) for source, target in pairs]


def ring_pairs(axis, distance):
    count = lax.axis_size(axis)
    return [(i, (i + distance) % count) for i in range(count)]


def base_taps(sides, step, row_count):
    blocks, here = lax.axis_size("seq"), lax.axis_index("seq")
    low = step * row_count
    even, middle, odd = [ref[:, low : low + row_count] for ref in sides]
    second = lax.rem(here, 2) == 1
    below, above = jnp.where(second, even, odd), jnp.where(second, odd, even)
    bases = jnp.concatenate([below, middle, above], axis=1)
    width, span = 3 * row_count, row_count + 2 * DILATION
    spread = jnp.broadcast_to(bases, (16, width))
    start = width - (row_count - DILATION + 8)
    taps = pltpu.roll(spread, start, 1, stride=1, stride_axis=0)[:, :span]
    place = lax.broadcasted_iota(jnp.int32, (16, span), 1) + (here * row_count - DILATION)
    source = place + 8 - lax.broadcasted_iota(jnp.int32, (16, span), 0)
    length = blocks * row_count
    inside = (place >= 0) & (place < length) & (source >= 0) & (source < length)
    return jnp.where(inside, taps, -1).astype(jnp.float32).astype(jnp.bfloat16)


def one_hot(taps, second):
    row = lax.broadcasted_iota(jnp.int32, (TABLE, 16), 0) // KINDS
    column = lax.broadcasted_iota(jnp.int32, (TABLE, 16), 1)
    chosen = (column == 15 - row + second * (2 * row - 14)).astype(jnp.float32)
    values = jnp.dot(chosen.astype(jnp.bfloat16), taps, preferred_element_type=jnp.float32)
    base = lax.broadcasted_iota(jnp.int32, values.shape, 0) % KINDS
    base = base + second * (KINDS - 1 - 2 * base)
    return (values == base.astype(jnp.float32)).astype(jnp.float32).T


def gelu(x):
    inner = x * (0.7978845608028654 + 0.035677408136300125 * (x * x))
    half = 0.5 * x
    return half + half * jnp.tanh(inner)


def activate(hot, gain_ref, pack_ref, act_ref):
    depth, width = act_ref.shape[1], gain_ref.shape[0]
    turn = lax.rem(width - lax.axis_index("dp") * depth, width)
    gain = jnp.broadcast_to(gain_ref[...].reshape(1, width), (8, width))
    gain = pltpu.roll(gain, turn, 1)[:1, :depth]
    tables = [pack_ref[rows] for rows in table_rows(depth, width, pack_ref.shape[1])]
    for start in range(0, hot.shape[0], ROW_STEP):
        rows = hot[start : start + ROW_STEP]
        parts = [jnp.dot(rows, table, preferred_element_type=jnp.float32) for table in tables]
        mean = sum(jnp.sum(part * part, axis=-1, keepdims=True) for part in parts) * (1.0 / width)
        scaled = parts[0][:, :depth] * lax.rsqrt(mean + EPS) * gain
        act_ref[start : start + ROW_STEP] = gelu(scaled).astype(jnp.bfloat16)


def convolve(blocks, pack_ref, copies=()):
    second = lax.axis_index("strand")
    depth = blocks[0].shape[1]
    total = None
    for row_block in EARLY_TAPS + LATE_TAPS:
        if row_block in LATE_TAPS:
            for copy in copies:
                copy.wait()
            copies = ()
        weight = pack_ref[row_block * depth : (row_block + 1) * depth]
        if row_block == 1:
            block = blocks[1]
        else:
            block = jnp.where(second == 1, blocks[2 - row_block], blocks[row_block])
        part = jnp.dot(block, weight, preferred_element_type=jnp.float32)
        total = part if total is None else total + part
    return total


def table_rows(depth, width, columns):
    first = 3 * depth
    count = width // columns
    return [slice(first + i * TABLE, first + (i + 1) * TABLE) for i in range(count)]


def plain_rows(depth, width, columns):
    first = 3 * depth + width // columns * TABLE
    return slice(first, first + TABLE)


def slice_kernel(point_any, tok_any, piece_ref, tok_ref, sems):
    rows, columns = piece_ref.shape
    low = pl.multiple_of(lax.axis_index("groups") * rows, 16)
    left = pl.multiple_of(lax.axis_index("strand") * columns, 128)
    part = point_any.at[pl.ds(low, rows), pl.ds(left, columns)]
    copies = [
        pltpu.make_async_copy(part, piece_ref, sems.at[0]),
        pltpu.make_async_copy(tok_any, tok_ref, sems.at[1]),
    ]
    for copy in copies:
        copy.start()
    for copy in copies:
        copy.wait()


def join_kernel(*refs):
    refs[-1][...] = jnp.concatenate([ref[...] for ref in refs[:-1]], axis=1)


def load_kernel(stem_any, w_any, pack_ref, stem_ref, flat_ref, sem, sems):
    depth, columns = w_any.shape[1:]
    copies = [pltpu.make_async_copy(stem_any, stem_ref, sem)]
    copies += weight_copies(w_any, pack_ref, EARLY_TAPS, sems)
    for copy in copies:
        copy.start()
    copies[0].wait()
    taps, kinds, width = stem_ref.shape
    slabs = [stem_ref[tap].astype(jnp.float32) for tap in range(taps)]
    slabs += [jnp.zeros((kinds, width), jnp.float32)] * (16 - taps)
    flat = jnp.concatenate(slabs)
    flat_ref[...] = flat.astype(jnp.bfloat16)
    me = lax.axis_index("dp")
    if depth == columns:
        parts = [lax.rem(me + index, width // columns) for index in range(width // columns)]
        starts = [pl.multiple_of(part * columns, 128) for part in parts]
        turned = [flat_ref[:, pl.ds(start, columns)] for start in starts]
    else:
        whole = pltpu.roll(flat, lax.rem(width - me * depth, width), 1).astype(jnp.bfloat16)
        turned = jnp.split(whole, width // columns, axis=1)
    for rows, part in zip(table_rows(depth, width, columns), turned):
        pack_ref[rows] = part
    column = pl.multiple_of(lax.axis_index("strand") * columns, 128)
    pack_ref[plain_rows(depth, width, columns)] = flat_ref[:, pl.ds(column, columns)]
    for copy in copies[1:]:
        copy.wait()


def weight_parts(weight, taps):
    rows = weight.shape[1] // 2
    return [(tap, low, rows) for tap in taps for low in (0, rows)]


def weight_copies(w_any, pack_ref, taps, sems):
    depth = w_any.shape[1]
    return [
        pltpu.make_async_copy(
            w_any.at[tap, pl.ds(low, rows)],
            pack_ref.at[pl.ds(tap * depth + low, rows)],
            sems.at[index],
        )
        for index, (tap, low, rows) in enumerate(weight_parts(w_any, taps))
    ]


def chunk_kernel(step, low, size, row_count, out_index, loading, *refs):
    gain_ref, pack_ref = refs[3:5]
    out_ref, act_ref = refs[out_index], refs[out_index + 2 if loading else -1]
    copies = []
    if loading:
        pack_ref = refs[out_index + 1]
        copies = weight_copies(refs[5], pack_ref, LATE_TAPS, refs[-1])
    for copy in copies:
        copy.start()
    taps = base_taps(refs[:3], step, row_count)
    hot = one_hot(taps, lax.axis_index("strand"))
    blocks = row_count // DILATION
    pieces = [hot[b * DILATION + low :][:size] for b in range(blocks + 2)]
    activate(jnp.concatenate(pieces).astype(jnp.bfloat16), gain_ref, pack_ref, act_ref)
    parts = [act_ref[t * size : (t + blocks) * size] for t in range(3)]
    out_ref[...] = convolve(parts, pack_ref, copies).astype(jnp.bfloat16)


def rows_of(ref, low, size):
    starts = range(low, ref.shape[0], DILATION)
    return jnp.concatenate([ref[start : start + size] for start in starts])


def middle_of(own_ref, gain_ref, parts, low, size):
    total = rows_of(own_ref, low, size)
    for ref in parts:
        total = total + ref[...].astype(jnp.float32)
    mean = jnp.mean(total * total, axis=-1, keepdims=True)
    return gelu(total * lax.rsqrt(mean + EPS) * gain_ref[...].reshape(1, -1)).astype(
        jnp.bfloat16
    )


def own_kernel(places, piece_rows, *refs):
    gain_ref, pack_ref = refs[3:5]
    pieces = refs[6 : 6 + len(places)]
    out_ref, res_ref, point_ref, act_ref, sems = refs[6 + len(places) :]
    ranks, groups = lax.axis_size("dp"), lax.axis_size("groups")
    me, group = lax.axis_index("dp"), lax.axis_index("groups")
    copies = []
    for index, (step, turn) in enumerate(places):
        place = lax.rem(me + step, ranks) * (piece_rows * groups)
        if step:
            place = place + lax.rem(group + turn, groups) * piece_rows
        source = pieces[index]
        if not step:
            columns = point_ref.shape[1]
            left = pl.multiple_of(lax.axis_index("strand") * columns, 128)
            source = source.at[:, pl.ds(left, columns)]
        target = pl.ds(pl.multiple_of(place, 16), source.shape[0])
        copies.append(pltpu.make_async_copy(source, point_ref.at[target], sems.at[index]))
        copies[-1].start()
    row_count = out_ref.shape[0]
    second = lax.axis_index("strand")
    taps = base_taps(refs[:3], 0, row_count)
    hot = one_hot(taps, second)
    here = slice(DILATION, DILATION + row_count)
    both = (hot[here] + one_hot(taps[:, here], 1 - second)).astype(jnp.bfloat16)
    plain = pack_ref[plain_rows(act_ref.shape[1], gain_ref.shape[0], pack_ref.shape[1])]
    res_ref[...] = jnp.dot(both, plain, preferred_element_type=jnp.float32)
    activate(hot.astype(jnp.bfloat16), gain_ref, pack_ref, act_ref)
    blocks = [act_ref[t * DILATION : t * DILATION + row_count] for t in range(3)]
    out_ref[...] = convolve(blocks, pack_ref)
    for copy in copies:
        copy.wait()


def middle_kernel(chunks, count, own_ref, gain_ref, *refs):
    out_ref = refs[-1]
    first, total_size = chunks[0][0], sum(size for _, size in chunks)
    for index, (low, size) in enumerate(chunks):
        parts = refs[index * count : (index + 1) * count]
        value = middle_of(own_ref, gain_ref, parts, low, size)
        for block in range(own_ref.shape[0] // DILATION):
            start = block * total_size + low - first
            out_ref[start : start + size] = value[block * size : (block + 1) * size]


def final_kernel(low, size, mine_ref, other_ref, res_ref, point_ref, *refs):
    out_ref = refs[-1]
    total = mine_ref[...].astype(jnp.float32) + other_ref[...].astype(jnp.float32)
    branch = jnp.dot(
        total.astype(jnp.bfloat16), point_ref[...], preferred_element_type=jnp.float32
    )
    value = (0.5 * (branch + rows_of(res_ref, low, size))).astype(jnp.bfloat16)
    out_ref[...] = value.reshape(out_ref.shape)


def in_hbm(x):
    return pltpu.with_memory_space_constraint(x, pltpu.HBM)


def cost(kind):
    return pl.CostEstimate(
        flops=int(1e9 * FLOPS[kind]), bytes_accessed=2**20, transcendentals=0
    )


def per_device(tokens, stem_table, conv_weight, gain_in, gain_mid, point_weight):
    row_count = tokens.shape[1]
    width = stem_table.shape[2]
    depth, inner = conv_weight.shape[1:]
    count, groups = lax.axis_size("dp"), lax.axis_size("groups")
    half = width // 2
    vmem = pl.BlockSpec(memory_space=pltpu.VMEM)
    anywhere = pl.BlockSpec(memory_space=pl.ANY)
    bf16, f32 = jnp.bfloat16, jnp.float32
    params = pltpu.CompilerParams(vmem_limit_bytes=24 * MIB)

    others = [lax.ppermute(tokens, "dp", ring_pairs("dp", -step)) for step in range(1, count)]
    piece_rows = point_weight.shape[0] // groups
    piece, here = pl.pallas_call(
        slice_kernel,
        out_shape=[
            jax.ShapeDtypeStruct((piece_rows, half), bf16),
            jax.ShapeDtypeStruct(tokens.shape, tokens.dtype),
        ],
        in_specs=[anywhere] * 2,
        out_specs=[vmem] * 2,
        scratch_shapes=[pltpu.SemaphoreType.DMA((2,))],
        compiler_params=params,
        cost_estimate=cost("early"),
        name="point_slice",
    )(in_hbm(point_weight), in_hbm(tokens))
    joined = pl.pallas_call(
        join_kernel,
        out_shape=jax.ShapeDtypeStruct((1, count * row_count), tokens.dtype),
        in_specs=[vmem] * count,
        out_specs=vmem,
        compiler_params=params,
        cost_estimate=cost("early"),
        name="join",
    )(here, *others)
    even = lax.ppermute(joined, "seq", pair_pairs("seq", 0))
    odd = lax.ppermute(joined, "seq", pair_pairs("seq", 1))
    pack_rows = 3 * depth + (width // inner + 1) * TABLE
    pack = pl.pallas_call(
        load_kernel,
        out_shape=jax.ShapeDtypeStruct((pack_rows, inner), bf16),
        in_specs=[anywhere] * 2,
        out_specs=vmem,
        scratch_shapes=[
            pltpu.VMEM(stem_table.shape, bf16),
            pltpu.VMEM((TABLE, width), bf16),
            pltpu.SemaphoreType.DMA,
            pltpu.SemaphoreType.DMA((len(weight_parts(conv_weight, EARLY_TAPS)),)),
        ],
        compiler_params=params,
        cost_estimate=cost("load"),
        name="load",
    )(in_hbm(stem_table), in_hbm(conv_weight))
    crossed = [lax.ppermute(piece, "dp", ring_pairs("dp", -step)) for step in range(1, count)]

    received = [[] for _ in CHUNKS]
    for step in range(1, count):
        for index, (low, size) in enumerate(CHUNKS):
            rows = row_count // DILATION * size
            loading, passing = step == 1 and index == 0, index == 1
            operands = [even, joined, odd, gain_in, pack]
            shapes = [jax.ShapeDtypeStruct((rows, inner), bf16)]
            scratch = [pltpu.VMEM((rows + 2 * size, depth), bf16)]
            aliases = {}
            if loading:
                operands.append(in_hbm(conv_weight))
                shapes.append(jax.ShapeDtypeStruct(pack.shape, bf16))
                late = len(weight_parts(conv_weight, LATE_TAPS))
                scratch.append(pltpu.SemaphoreType.DMA((late,)))
                aliases = {4: 1}
            if passing:
                operands.append(crossed[step - 1])
                shapes.append(jax.ShapeDtypeStruct(crossed[step - 1].shape, bf16))
                aliases = {5: 1}
            if index:
                operands.append(part)
            part, *passed = pl.pallas_call(
                functools.partial(
                    chunk_kernel, step, low, size, row_count, len(operands), loading
                ),
                out_shape=shapes,
                in_specs=[vmem] * 5 + [anywhere] * (len(operands) - 5),
                out_specs=[vmem, vmem if loading else anywhere][: len(shapes)],
                scratch_shapes=scratch,
                input_output_aliases=aliases,
                compiler_params=params,
                cost_estimate=cost(f"sent{index}"),
                name="conv_sent",
            )(*operands)
            if loading:
                pack = passed.pop()
            if passed:
                crossed[step - 1] = passed[0]
            received[index].append(lax.ppermute(part, "dp", ring_pairs("dp", step)))

    places, pieces = [(0, 0)], [in_hbm(point_weight)]
    for step in range(1, count):
        for turn in range(groups):
            piece = crossed[step - 1]
            if turn:
                piece = lax.ppermute(piece, "groups", ring_pairs("groups", -turn))
            places.append((step, turn))
            pieces.append(piece)

    own, res, point = pl.pallas_call(
        functools.partial(own_kernel, places, piece_rows),
        out_shape=[
            jax.ShapeDtypeStruct((row_count, inner), f32),
            jax.ShapeDtypeStruct((row_count, half), f32),
            jax.ShapeDtypeStruct((inner, half), bf16),
        ],
        in_specs=[vmem] * 5 + [anywhere] * (1 + len(pieces)),
        out_specs=[vmem] * 3,
        scratch_shapes=[
            pltpu.VMEM((row_count + 2 * DILATION, depth), bf16),
            pltpu.SemaphoreType.DMA((len(pieces),)),
        ],
        compiler_params=params,
        cost_estimate=cost("own"),
        name="conv_own",
    )(even, joined, odd, gain_in, pack, part, *pieces)

    out = None
    blocks = row_count // DILATION
    for index, tail in enumerate(TAILS):
        chunks = [CHUNKS[chunk] for chunk in tail]
        low, size = chunks[0][0], sum(size for _, size in chunks)
        parts = [part for chunk in tail for part in received[chunk]]
        middle = pl.pallas_call(
            functools.partial(middle_kernel, chunks, count - 1),
            out_shape=jax.ShapeDtypeStruct((blocks * size, inner), bf16),
            in_specs=[vmem] * (2 + len(parts)),
            out_specs=vmem,
            compiler_params=params,
            cost_estimate=cost(f"middle{index}"),
            name="middle",
        )(own, gain_mid, *parts)
        other = lax.ppermute(middle, "strand", ring_pairs("strand", 1))
        operands = [middle, other, res, point] + ([] if out is None else [out])
        out = pl.pallas_call(
            functools.partial(final_kernel, low, size),
            grid=(1,),
            out_shape=jax.ShapeDtypeStruct((blocks, DILATION, half), bf16),
            in_specs=[vmem] * 4 + [anywhere] * (len(operands) - 4),
            out_specs=pl.BlockSpec((blocks, size, half), lambda i, at=low // size: (0, at, 0)),
            input_output_aliases={} if out is None else {4: 0},
            compiler_params=params,
            cost_estimate=cost(f"final{index}"),
            name="final",
        )(*operands)
    return out.reshape(1, row_count, half)


def solution(mesh):
    return jax.shard_map(
        per_device,
        mesh=mesh,
        in_specs=(P(("groups", "dp"), "seq"), P(), P(None, "dp", None), P(), P(), P("dp", None)),
        out_specs=P(("groups", "dp"), "seq", "strand"),
        check_vma=False,
    )
```

profile of v0, /device:TPU:9, one launch (start us, length us, event | category | flops | bytes accessed | tf_op | source)
XLA Modules:
  0.0 33.8 jit_solution(14769932580762301385)
XLA Ops:
  0.0 1.2 %collective-permute-start = (s32[1,512]{1,0:T(1,128)}, s32[1,512]{1,0:T(1,128)S(1)}, u32[]{:S(2)}, u32[]{:S(2)}) collective-permute-start(s32[1,512]{1,0:T(1,128)} %tok_any.1), channel_id=1, source_target_pairs={{0,2},{2,0},{1,3},{3,1},{4,6},{6,4},{5,7},{7,5},{8,10},{10,8},{9,1... | collective-permute-start | bytes 6152 | tf_op jit(solution)/shard_map/ppermute | solution.py:295
  1.2 1.0 %point_slice.1 = (bf16[192,768]{1,0:T(8,128)(2,1)S(1)}, s32[1,512]{1,0:T(1,128)S(1)}) custom-call(bf16[384,1536]{1,0:T(8,128)(2,1)} %refs_6_.1, s32[1,512]{1,0:T(1,128)} %tok_any.1), custom_call_target="tpu_custom_call" | custom-call | flops 100000000 | bytes 1048576 | tf_op jit(solution)/shard_map/point_slice/pallas_call | solution.py:297
  2.2 0.3 collective-permute-start.3
  2.5 0.1 collective-permute-done.refs_1_
  2.7 0.1 collective-permute-start.1
  2.7 4.5 %collective-permute-start.2 = (s32[1,1024]{1,0:T(1,128)S(1)}, s32[1,1024]{1,0:T(1,128)S(1)}, u32[]{:S(2)}, u32[]{:S(2)}) collective-permute-start(s32[1,1024]{1,0:T(1,128)S(1)} %join.1.refs_1_), channel_id=1, source_target_pairs={{4,8},{8,4},{5,9},{9,5},{6,10},{10,6},{7,11},{11,7},{20,24},{24,20... | collective-permute-start | bytes 12296 | tf_op jit(solution)/shard_map/ppermute | solution.py:320
  7.2 1.7 %load.1.refs_4_ = bf16[2496,768]{1,0:T(8,128)(2,1)S(1)} custom-call(bf16[15,4,1536]{2,1,0:T(4,128)(2,1)} %stem_any.1, bf16[3,768,768]{2,1,0:T(8,128)(2,1)} %refs_5_.1), custom_call_target="tpu_custom_call" | custom-call | flops 100000000 | bytes 1048576 | tf_op jit(solution)/shard_map/load/pallas_call | solution.py:322
  9.0 1.9 %conv_sent.3 = (bf16[192,768]{1,0:T(8,128)(2,1)S(1)}, bf16[2496,768]{1,0:T(8,128)(2,1)S(1)}) custom-call(s32[1,1024]{1,0:T(1,128)S(1)} %collective-permute-done.1.refs_0_, s32[1,1024]{1,0:T(1,128)S(1)} %join.1.refs_1_, s32[1,1024]{1,0:T(1,128)S(1)} %collective-permute-done.2.refs_2_, f32[1536]{0:T(1024)S(1)} %copy-done, ...), custom_call_target="tpu_custom_call", output_to_operand_aliasing={{1}: (4, {})} | custom-call | flops 15000000512 | bytes 1048576 | tf_op jit(solution)/shard_map/conv_sent/pallas_call | solution.py:360
  10.9 1.3 %collective-permute-start.7 = (bf16[192,768]{1,0:T(8,128)(2,1)S(1)}, bf16[192,768]{1,0:T(8,128)(2,1)S(1)}, u32[]{:S(2)}, u32[]{:S(2)}) collective-permute-start(bf16[192,768]{1,0:T(8,128)(2,1)S(1)} %get-tuple-element.17.refs_6_), channel_id=1, source_target_pairs={{0,2},{2,0},{1,3},{3,1},{4,6},{6,4},{5,7},{7,5},{8,10},{10,8},{9,1... | collective-permute-start | bytes 884744 | tf_op jit(solution)/shard_map/ppermute | solution.py:377
  12.2 1.9 %conv_sent.4 = (bf16[192,768]{1,0:T(8,128)(2,1)S(1)}, bf16[192,768]{1,0:T(8,128)(2,1)S(1)}) custom-call(s32[1,1024]{1,0:T(1,128)S(1)} %collective-permute-done.1.refs_0_, s32[1,1024]{1,0:T(1,128)S(1)} %join.1.refs_1_, s32[1,1024]{1,0:T(1,128)S(1)} %collective-permute-done.2.refs_2_, f32[1536]{0:T(1024)S(1)} %copy-done, ...), custom_call_target="tpu_custom_call", output_to_operand_aliasing={{1}: (5, {})} | custom-call | flops 500000000 | bytes 1048576 | tf_op jit(solution)/shard_map/conv_sent/pallas_call | solution.py:360
  14.1 1.3 %collective-permute-start.4 = (bf16[192,768]{1,0:T(8,128)(2,1)S(1)}, bf16[192,768]{1,0:T(8,128)(2,1)S(1)}, u32[]{:S(2)}, u32[]{:S(2)}) collective-permute-start(bf16[192,768]{1,0:T(8,128)(2,1)S(1)} %get-tuple-element.19.refs_7_), channel_id=1, source_target_pairs={{0,16},{16,0},{1,17},{17,1},{2,18},{18,2},{3,19},{19,3},{4,20},{20... | collective-permute-start | bytes 884744 | tf_op jit(solution)/shard_map/ppermute | solution.py:384
  15.4 0.3 collective-permute-start.8
  15.6 1.6 %conv_sent.5.refs_5_ = bf16[128,768]{1,0:T(8,128)(2,1)S(1)} custom-call(s32[1,1024]{1,0:T(1,128)S(1)} %collective-permute-done.1.refs_0_, s32[1,1024]{1,0:T(1,128)S(1)} %join.1.refs_1_, s32[1,1024]{1,0:T(1,128)S(1)} %collective-permute-done.2.refs_2_, f32[1536]{0:T(1024)S(1)} %copy-done, bf16[2496,768]{1,0:T(8,128)(2,1)S(1)} %get-tuple-element.15.refs_4_, ...), custom_call_target="tpu_custom_call" | custom-call | flops 15000000512 | bytes 1048576 | tf_op jit(solution)/shard_map/conv_sent/pallas_call | solution.py:360
  17.3 0.0 copy-start.1
  17.3 1.3 %collective-permute-start.5 = (bf16[128,768]{1,0:T(8,128)(2,1)S(1)}, bf16[128,768]{1,0:T(8,128)(2,1)S(1)}, u32[]{:S(2)}, u32[]{:S(2)}) collective-permute-start(bf16[128,768]{1,0:T(8,128)(2,1)S(1)} %conv_sent.5.refs_5_), channel_id=1, source_target_pairs={{0,2},{2,0},{1,3},{3,1},{4,6},{6,4},{5,7},{7,5},{8,10},{10,8},{9,1... | collective-permute-start | bytes 589832 | tf_op jit(solution)/shard_map/ppermute | solution.py:377
  18.6 1.4 %collective-permute-done.4.refs_8_ = bf16[192,768]{1,0:T(8,128)(2,1)S(1)} collective-permute-done((bf16[192,768]{1,0:T(8,128)(2,1)S(1)}, bf16[192,768]{1,0:T(8,128)(2,1)S(1)}, u32[]{:S(2)}, u32[]{:S(2)}) %collective-permute-start.4) | collective-permute-done | bytes 294944 | tf_op jit(solution)/shard_map/ppermute | solution.py:384
  20.0 4.4 %conv_own.1 = (f32[512,768]{1,0:T(8,128)S(1)}, f32[512,768]{1,0:T(8,128)S(1)}, bf16[768,768]{1,0:T(8,128)(2,1)S(1)}) custom-call(s32[1,1024]{1,0:T(1,128)S(1)} %collective-permute-done.1.refs_0_, s32[1,1024]{1,0:T(1,128)S(1)} %join.1.refs_1_, s32[1,1024]{1,0:T(1,128)S(1)} %collective-permute-done.2.refs_2_, f32[1536]{0:T(1024)S(1)} %copy-done, ...), custom_call_target="tpu_custom_call" | custom-call | flops 15000000512 | bytes 1048576 | tf_op jit(solution)/shard_map/conv_own/pallas_call | solution.py:388
  24.4 0.0 collective-permute-done.8.refs_1_
  24.5 0.6 %middle.3.mine_ref = bf16[384,768]{1,0:T(8,128)(2,1)S(1)} custom-call(f32[512,768]{1,0:T(8,128)S(1)} %get-tuple-element.20.own_ref, f32[768]{0:T(1024)S(1)} %copy-done.1, bf16[192,768]{1,0:T(8,128)(2,1)S(1)} %collective-permute-done.7.refs_0_, bf16[192,768]{1,0:T(8,128)(2,1)S(1)} %collective-permute-done.8.refs_1_), custom_call_target="tpu_custom_call" | custom-call | flops 50000000 | bytes 1048576 | tf_op jit(solution)/shard_map/middle/pallas_call | solution.py:412
  25.0 4.2 %collective-permute-start.9 = (bf16[384,768]{1,0:T(8,128)(2,1)S(1)}, bf16[384,768]{1,0:T(8,128)(2,1)S(1)}, u32[]{:S(2)}, u32[]{:S(2)}) collective-permute-start(bf16[384,768]{1,0:T(8,128)(2,1)S(1)} %middle.3.mine_ref), channel_id=1, source_target_pairs={{0,1},{1,0},{2,3},{3,2},{4,5},{5,4},{6,7},{7,6},{8,9},{9,8},{10,11... | collective-permute-start | bytes 1769480 | tf_op jit(solution)/shard_map/ppermute | solution.py:421
  29.3 0.2 middle.2.mine_ref
  29.5 1.7 %collective-permute-start.6 = (bf16[128,768]{1,0:T(8,128)(2,1)S(1)}, bf16[128,768]{1,0:T(8,128)(2,1)S(1)}, u32[]{:S(2)}, u32[]{:S(2)}) collective-permute-start(bf16[128,768]{1,0:T(8,128)(2,1)S(1)} %middle.2.mine_ref), channel_id=1, source_target_pairs={{0,1},{1,0},{2,3},{3,2},{4,5},{5,4},{6,7},{7,6},{8,9},{9,8},{10,11... | collective-permute-start | bytes 589832 | tf_op jit(solution)/shard_map/ppermute | solution.py:421
  31.3 1.5 %final.2.refs_0_ = bf16[2,256,768]{2,1,0:T(8,128)(2,1)} custom-call(bf16[384,768]{1,0:T(8,128)(2,1)S(1)} %middle.3.mine_ref, bf16[384,768]{1,0:T(8,128)(2,1)S(1)} %collective-permute-done.9.other_ref, f32[512,768]{1,0:T(8,128)S(1)} %get-tuple-element.21.res_ref, bf16[768,768]{1,0:T(8,128)(2,1)S(1)} %get-tuple-element.22.point_ref), custom_call_target="tpu_custom_call" | custom-call | flops 500000000 | bytes 1048576 | tf_op jit(solution)/shard_map/final/pallas_call | solution.py:423
  32.7 1.0 %final.3 = bf16[2,256,768]{2,1,0:T(8,128)(2,1)} custom-call(bf16[128,768]{1,0:T(8,128)(2,1)S(1)} %middle.2.mine_ref, bf16[128,768]{1,0:T(8,128)(2,1)S(1)} %collective-permute-done.6.other_ref, f32[512,768]{1,0:T(8,128)S(1)} %get-tuple-element.21.res_ref, bf16[768,768]{1,0:T(8,128)(2,1)S(1)} %get-tuple-element.22.point_ref, ...), custom_call_target="tpu_custom_call", output_to_operand_aliasing={{}: (4, {})} | custom-call | flops 15000000512 | bytes 1048576 | tf_op jit(solution)/shard_map/final/pallas_call | solution.py:423
  (11 shorter events, 0.0 us)
Async XLA Ops:
  0.0 2.6 %collective-permute-start = (s32[1,512]{1,0:T(1,128)}, s32[1,512]{1,0:T(1,128)S(1)}, u32[]{:S(2)}, u32[]{:S(2)}) collective-permute-start(s32[1,512]{1,0:T(1,128)} %tok_any.1), channel_id=1, source_target_pairs={{0,2},{2,0},{1,3},{3,1},{4,6},{6,4},{5,7},{7,5},{8,10},{10,8},{9,1... | collective-permute-start | bytes 6152 | tf_op jit(solution)/shard_map/ppermute | solution.py:295
  2.2 10.0 %collective-permute-start.3 = (bf16[192,768]{1,0:T(8,128)(2,1)S(1)}, bf16[192,768]{1,0:T(8,128)(2,1)S(1)}, u32[]{:S(2)}, u32[]{:S(2)}) collective-permute-start(bf16[192,768]{1,0:T(8,128)(2,1)S(1)} %get-tuple-element.16), channel_id=1, source_target_pairs={{0,2},{2,0},{1,3},{3,1},{4,6},{6,4},{5,7},{7,5},{8,10},{10,8},{9,1... | collective-permute-start | bytes 884744 | tf_op jit(solution)/shard_map/ppermute | solution.py:337
  2.7 6.3 %copy-start = (f32[1536]{0:T(1024)S(1)}, f32[1536]{0:T(1024)}, u32[]{:S(2)}) copy-start(f32[1536]{0:T(1024)} %refs_3_.7) | copy-start | bytes 18436
  2.7 6.3 %collective-permute-start.1 = (s32[1,1024]{1,0:T(1,128)S(1)}, s32[1,1024]{1,0:T(1,128)S(1)}, u32[]{:S(2)}, u32[]{:S(2)}) collective-permute-start(s32[1,1024]{1,0:T(1,128)S(1)} %join.1.refs_1_), channel_id=1, source_target_pairs={{0,4},{8,12},{4,0},{12,8},{1,5},{9,13},{5,1},{13,9},{2,6},{10,14},... | collective-permute-start | bytes 12296 | tf_op jit(solution)/shard_map/ppermute | solution.py:319
  2.7 6.2 %collective-permute-start.2 = (s32[1,1024]{1,0:T(1,128)S(1)}, s32[1,1024]{1,0:T(1,128)S(1)}, u32[]{:S(2)}, u32[]{:S(2)}) collective-permute-start(s32[1,1024]{1,0:T(1,128)S(1)} %join.1.refs_1_), channel_id=1, source_target_pairs={{4,8},{8,4},{5,9},{9,5},{6,10},{10,6},{7,11},{11,7},{20,24},{24,20... | collective-permute-start | bytes 12296 | tf_op jit(solution)/shard_map/ppermute | solution.py:320
  10.9 13.5 %collective-permute-start.7 = (bf16[192,768]{1,0:T(8,128)(2,1)S(1)}, bf16[192,768]{1,0:T(8,128)(2,1)S(1)}, u32[]{:S(2)}, u32[]{:S(2)}) collective-permute-start(bf16[192,768]{1,0:T(8,128)(2,1)S(1)} %get-tuple-element.17.refs_6_), channel_id=1, source_target_pairs={{0,2},{2,0},{1,3},{3,1},{4,6},{6,4},{5,7},{7,5},{8,10},{10,8},{9,1... | collective-permute-start | bytes 884744 | tf_op jit(solution)/shard_map/ppermute | solution.py:377
  14.1 5.9 %collective-permute-start.4 = (bf16[192,768]{1,0:T(8,128)(2,1)S(1)}, bf16[192,768]{1,0:T(8,128)(2,1)S(1)}, u32[]{:S(2)}, u32[]{:S(2)}) collective-permute-start(bf16[192,768]{1,0:T(8,128)(2,1)S(1)} %get-tuple-element.19.refs_7_), channel_id=1, source_target_pairs={{0,16},{16,0},{1,17},{17,1},{2,18},{18,2},{3,19},{19,3},{4,20},{20... | collective-permute-start | bytes 884744 | tf_op jit(solution)/shard_map/ppermute | solution.py:384
  15.4 9.1 %collective-permute-start.8 = (bf16[192,768]{1,0:T(8,128)(2,1)S(1)}, bf16[192,768]{1,0:T(8,128)(2,1)S(1)}, u32[]{:S(2)}, u32[]{:S(2)}) collective-permute-start(bf16[192,768]{1,0:T(8,128)(2,1)S(1)} %get-tuple-element.18.refs_5_), channel_id=1, source_target_pairs={{0,2},{2,0},{1,3},{3,1},{4,6},{6,4},{5,7},{7,5},{8,10},{10,8},{9,1... | collective-permute-start | bytes 884744 | tf_op jit(solution)/shard_map/ppermute | solution.py:377
  17.3 7.2 %copy-start.1 = (f32[768]{0:T(1024)S(1)}, f32[768]{0:T(1024)}, u32[]{:S(2)}) copy-start(f32[768]{0:T(1024)} %gain_ref.3) | copy-start | bytes 9220
  17.3 12.0 %collective-permute-start.5 = (bf16[128,768]{1,0:T(8,128)(2,1)S(1)}, bf16[128,768]{1,0:T(8,128)(2,1)S(1)}, u32[]{:S(2)}, u32[]{:S(2)}) collective-permute-start(bf16[128,768]{1,0:T(8,128)(2,1)S(1)} %conv_sent.5.refs_5_), channel_id=1, source_target_pairs={{0,2},{2,0},{1,3},{3,1},{4,6},{6,4},{5,7},{7,5},{8,10},{10,8},{9,1... | collective-permute-start | bytes 589832 | tf_op jit(solution)/shard_map/ppermute | solution.py:377
  25.0 6.2 %collective-permute-start.9 = (bf16[384,768]{1,0:T(8,128)(2,1)S(1)}, bf16[384,768]{1,0:T(8,128)(2,1)S(1)}, u32[]{:S(2)}, u32[]{:S(2)}) collective-permute-start(bf16[384,768]{1,0:T(8,128)(2,1)S(1)} %middle.3.mine_ref), channel_id=1, source_target_pairs={{0,1},{1,0},{2,3},{3,2},{4,5},{5,4},{6,7},{7,6},{8,9},{9,8},{10,11... | collective-permute-start | bytes 1769480 | tf_op jit(solution)/shard_map/ppermute | solution.py:421
  29.5 3.2 %collective-permute-start.6 = (bf16[128,768]{1,0:T(8,128)(2,1)S(1)}, bf16[128,768]{1,0:T(8,128)(2,1)S(1)}, u32[]{:S(2)}, u32[]{:S(2)}) collective-permute-start(bf16[128,768]{1,0:T(8,128)(2,1)S(1)} %middle.2.mine_ref), channel_id=1, source_target_pairs={{0,1},{1,0},{2,3},{3,2},{4,5},{5,4},{6,7},{7,6},{8,9},{9,8},{10,11... | collective-permute-start | bytes 589832 | tf_op jit(solution)/shard_map/ppermute | solution.py:421
where the time goes:
time: 33.9 us; the launch traced here: 33.8 us
  starting transfers between devices  16.1 us (47%)
  Pallas kernels  15.9 us (47%)
  waiting for transfers between devices  1.6 us (5%)
    ppermute x2, starting transfers between devices, per_device(): other = lax.ppermute(middle, 'strand', ring_pairs('strand', 1))  5.95 us
    pallas_call x3, Pallas kernels, per_device(): pl.pallas_call(functools.partial(chunk_kernel, step, low, size, row_count...  5.45 us
    ppermute x1, starting transfers between devices, per_device(): odd = lax.ppermute(joined, 'seq', pair_pairs('seq', 1))  4.48 us
    pallas_call x1, Pallas kernels, per_device(): pl.pallas_call(functools.partial(own_kernel, places, piece_rows), out_sha...  4.42 us
    ppermute x3, starting transfers between devices, per_device(): received[index].append(lax.ppermute(part, 'dp', ring_pairs('dp', step)))  2.81 us
    pallas_call x2, Pallas kernels, per_device(): pl.pallas_call(functools.partial(final_kernel, low, size), grid=(1,), out...  2.5 us
    pallas_call x1, Pallas kernels, per_device(): pl.pallas_call(load_kernel, out_shape=jax.ShapeDtypeStruct((pack_rows, in...  1.7 us
    ppermute x1, waiting for transfers between devices, per_device(): piece = lax.ppermute(piece, 'groups', ring_pairs('groups', -turn))  1.43 us
  transfers between devices with their start and end apart: 10, of which 2 were waited for; matrix products, arithmetic and copies ran while one was open for 0% of the time, Pallas kernels for 44%

commit v1 on v0

--- a/solution.py
+++ b/solution.py
@@ -9,7 +9,7 @@
 
 DILATION = 256
 EPS = 1e-06
-ROW_STEP = 128
+ROW_STEPS = (256, 192, 64)
 CHUNKS = ((0, 96), (96, 96), (192, 64))
 TAILS = ((0, 1), (2,))
 EARLY_TAPS, LATE_TAPS = (0, 1), (2,)
@@ -81,28 +81,27 @@
     gain = jnp.broadcast_to(gain_ref[...].reshape(1, width), (8, width))
     gain = pltpu.roll(gain, turn, 1)[:1, :depth]
     tables = [pack_ref[rows] for rows in table_rows(depth, width, pack_ref.shape[1])]
-    for start in range(0, hot.shape[0], ROW_STEP):
-        rows = hot[start : start + ROW_STEP]
+    step = next(step for step in ROW_STEPS if hot.shape[0] % step == 0)
+    for start in range(0, hot.shape[0], step):
+        rows = hot[start : start + step]
         parts = [jnp.dot(rows, table, preferred_element_type=jnp.float32) for table in tables]
-        mean = sum(jnp.sum(part * part, axis=-1, keepdims=True) for part in parts) * (1.0 / width)
+        square = sum(part * part for part in parts)
+        mean = jnp.sum(square, axis=-1, keepdims=True) * (1.0 / width)
         scaled = parts[0][:, :depth] * lax.rsqrt(mean + EPS) * gain
-        act_ref[start : start + ROW_STEP] = gelu(scaled).astype(jnp.bfloat16)
-
-
-def convolve(blocks, pack_ref, copies=()):
+        act_ref[start : start + step] = gelu(scaled).astype(jnp.bfloat16)
+
+
+def convolve(act_ref, size, rows, pack_ref, copies=()):
     second = lax.axis_index("strand")
-    depth = blocks[0].shape[1]
+    depth = act_ref.shape[1]
     total = None
-    for row_block in EARLY_TAPS + LATE_TAPS:
-        if row_block in LATE_TAPS:
+    for tap in EARLY_TAPS + LATE_TAPS:
+        if tap in LATE_TAPS:
             for copy in copies:
                 copy.wait()
-            copies = ()
-        weight = pack_ref[row_block * depth : (row_block + 1) * depth]
-        if row_block == 1:
-            block = blocks[1]
-        else:
-            block = jnp.where(second == 1, blocks[2 - row_block], blocks[row_block])
+        start = pl.multiple_of((tap + second * (2 - 2 * tap)) * size, 16)
+        block = act_ref[pl.ds(start, rows), :]
+        weight = pack_ref[tap * depth : (tap + 1) * depth]
         part = jnp.dot(block, weight, preferred_element_type=jnp.float32)
         total = part if total is None else total + part
     return total
@@ -197,8 +196,8 @@
     blocks = row_count // DILATION
     pieces = [hot[b * DILATION + low :][:size] for b in range(blocks + 2)]
     activate(jnp.concatenate(pieces).astype(jnp.bfloat16), gain_ref, pack_ref, act_ref)
-    parts = [act_ref[t * size : (t + blocks) * size] for t in range(3)]
-    out_ref[...] = convolve(parts, pack_ref, copies).astype(jnp.bfloat16)
+    total = convolve(act_ref, size, blocks * size, pack_ref, copies)
+    out_ref[...] = total.astype(jnp.bfloat16)
 
 
 def rows_of(ref, low, size):
@@ -244,8 +243,7 @@
     plain = pack_ref[plain_rows(act_ref.shape[1], gain_ref.shape[0], pack_ref.shape[1])]
     res_ref[...] = jnp.dot(both, plain, preferred_element_type=jnp.float32)
     activate(hot.astype(jnp.bfloat16), gain_ref, pack_ref, act_ref)
-    blocks = [act_ref[t * DILATION : t * DILATION + row_count] for t in range(3)]
-    out_ref[...] = convolve(blocks, pack_ref)
+    out_ref[...] = convolve(act_ref, DILATION, row_count, pack_ref)
     for copy in copies:
         copy.wait()
 

time: 33.9 us -> 34.2 us (level)
  the two profiles are of different devices: /device:TPU:9 before, /device:TPU:11 now
where the time goes in v1:
time: 34.2 us; the launch traced here: 34 us
  Pallas kernels  16.6 us (49%)
  starting transfers between devices  15.7 us (46%)
  waiting for transfers between devices  1.52 us (4%)
    ppermute x2, starting transfers between devices, per_device(): other = lax.ppermute(middle, 'strand', ring_pairs('strand', 1))  6.51 us
    pallas_call x3, Pallas kernels, per_device(): pl.pallas_call(functools.partial(chunk_kernel, step, low, size, row_count...  6.1 us
    pallas_call x1, Pallas kernels, per_device(): pl.pallas_call(functools.partial(own_kernel, places, piece_rows), out_sha...  4.52 us
    ppermute x1, starting transfers between devices, per_device(): odd = lax.ppermute(joined, 'seq', pair_pairs('seq', 1))  4.32 us
    pallas_call x2, Pallas kernels, per_device(): pl.pallas_call(functools.partial(final_kernel, low, size), grid=(1,), out...  2.5 us
    ppermute x3, starting transfers between devices, per_device(): received[index].append(lax.ppermute(part, 'dp', ring_pairs('dp', step)))  1.84 us
    pallas_call x1, Pallas kernels, per_device(): pl.pallas_call(load_kernel, out_shape=jax.ShapeDtypeStruct((pack_rows, in...  1.7 us
    ppermute x1, waiting for transfers between devices, per_device(): piece = lax.ppermute(piece, 'groups', ring_pairs('groups', -turn))  1.37 us
  transfers between devices with their start and end apart: 10, of which 2 were waited for; matrix products, arithmetic and copies ran while one was open for 0% of the time, Pallas kernels for 46%

profile of v1, /device:TPU:11, one launch (start us, length us, event | category | flops | bytes accessed | tf_op | source)
XLA Modules:
  0.0 34.0 jit_solution(3170097758252759019)
XLA Ops:
  0.0 0.3 collective-permute-start
  0.3 1.0 %point_slice.1 = (bf16[192,768]{1,0:T(8,128)(2,1)S(1)}, s32[1,512]{1,0:T(1,128)S(1)}) custom-call(bf16[384,1536]{1,0:T(8,128)(2,1)} %refs_6_.1, s32[1,512]{1,0:T(1,128)} %tok_any.1), custom_call_target="tpu_custom_call" | custom-call | flops 100000000 | bytes 1048576 | tf_op jit(solution)/shard_map/point_slice/pallas_call | solution.py:295
  1.2 1.3 %collective-permute-start.3 = (bf16[192,768]{1,0:T(8,128)(2,1)S(1)}, bf16[192,768]{1,0:T(8,128)(2,1)S(1)}, u32[]{:S(2)}, u32[]{:S(2)}) collective-permute-start(bf16[192,768]{1,0:T(8,128)(2,1)S(1)} %get-tuple-element.16), channel_id=1, source_target_pairs={{0,2},{2,0},{1,3},{3,1},{4,6},{6,4},{5,7},{7,5},{8,10},{10,8},{9,1... | collective-permute-start | bytes 884744 | tf_op jit(solution)/shard_map/ppermute | solution.py:335
  2.5 0.1 collective-permute-done.refs_1_
  2.7 0.2 collective-permute-start.1
  2.9 4.3 %collective-permute-start.2 = (s32[1,1024]{1,0:T(1,128)S(1)}, s32[1,1024]{1,0:T(1,128)S(1)}, u32[]{:S(2)}, u32[]{:S(2)}) collective-permute-start(s32[1,1024]{1,0:T(1,128)S(1)} %join.1.refs_1_), channel_id=1, source_target_pairs={{4,8},{8,4},{5,9},{9,5},{6,10},{10,6},{7,11},{11,7},{20,24},{24,20... | collective-permute-start | bytes 12296 | tf_op jit(solution)/shard_map/ppermute | solution.py:318
  7.2 1.7 %load.1.refs_4_ = bf16[2496,768]{1,0:T(8,128)(2,1)S(1)} custom-call(bf16[15,4,1536]{2,1,0:T(4,128)(2,1)} %stem_any.1, bf16[3,768,768]{2,1,0:T(8,128)(2,1)} %refs_5_.1), custom_call_target="tpu_custom_call" | custom-call | flops 100000000 | bytes 1048576 | tf_op jit(solution)/shard_map/load/pallas_call | solution.py:320
  8.9 0.0 collective-permute-done.1.refs_0_
  9.0 2.2 %conv_sent.3 = (bf16[192,768]{1,0:T(8,128)(2,1)S(1)}, bf16[2496,768]{1,0:T(8,128)(2,1)S(1)}) custom-call(s32[1,1024]{1,0:T(1,128)S(1)} %collective-permute-done.1.refs_0_, s32[1,1024]{1,0:T(1,128)S(1)} %join.1.refs_1_, s32[1,1024]{1,0:T(1,128)S(1)} %collective-permute-done.2.refs_2_, f32[1536]{0:T(1024)S(1)} %copy-done, ...), custom_call_target="tpu_custom_call", output_to_operand_aliasing={{1}: (4, {})} | custom-call | flops 15000000512 | bytes 1048576 | tf_op jit(solution)/shard_map/conv_sent/pallas_call | solution.py:358
  11.2 0.3 collective-permute-start.7
  11.5 2.2 %conv_sent.4 = (bf16[192,768]{1,0:T(8,128)(2,1)S(1)}, bf16[192,768]{1,0:T(8,128)(2,1)S(1)}) custom-call(s32[1,1024]{1,0:T(1,128)S(1)} %collective-permute-done.1.refs_0_, s32[1,1024]{1,0:T(1,128)S(1)} %join.1.refs_1_, s32[1,1024]{1,0:T(1,128)S(1)} %collective-permute-done.2.refs_2_, f32[1536]{0:T(1024)S(1)} %copy-done, ...), custom_call_target="tpu_custom_call", output_to_operand_aliasing={{1}: (5, {})} | custom-call | flops 500000000 | bytes 1048576 | tf_op jit(solution)/shard_map/conv_sent/pallas_call | solution.py:358
  13.7 1.3 %collective-permute-start.4 = (bf16[192,768]{1,0:T(8,128)(2,1)S(1)}, bf16[192,768]{1,0:T(8,128)(2,1)S(1)}, u32[]{:S(2)}, u32[]{:S(2)}) collective-permute-start(bf16[192,768]{1,0:T(8,128)(2,1)S(1)} %get-tuple-element.19.refs_7_), channel_id=1, source_target_pairs={{0,16},{16,0},{1,17},{17,1},{2,18},{18,2},{3,19},{19,3},{4,20},{20... | collective-permute-start | bytes 884744 | tf_op jit(solution)/shard_map/ppermute | solution.py:382
  15.0 1.2 %collective-permute-start.8 = (bf16[192,768]{1,0:T(8,128)(2,1)S(1)}, bf16[192,768]{1,0:T(8,128)(2,1)S(1)}, u32[]{:S(2)}, u32[]{:S(2)}) collective-permute-start(bf16[192,768]{1,0:T(8,128)(2,1)S(1)} %get-tuple-element.18.refs_5_), channel_id=1, source_target_pairs={{0,2},{2,0},{1,3},{3,1},{4,6},{6,4},{5,7},{7,5},{8,10},{10,8},{9,1... | collective-permute-start | bytes 884744 | tf_op jit(solution)/shard_map/ppermute | solution.py:375
  16.2 1.7 %conv_sent.5.refs_5_ = bf16[128,768]{1,0:T(8,128)(2,1)S(1)} custom-call(s32[1,1024]{1,0:T(1,128)S(1)} %collective-permute-done.1.refs_0_, s32[1,1024]{1,0:T(1,128)S(1)} %join.1.refs_1_, s32[1,1024]{1,0:T(1,128)S(1)} %collective-permute-done.2.refs_2_, f32[1536]{0:T(1024)S(1)} %copy-done, bf16[2496,768]{1,0:T(8,128)(2,1)S(1)} %get-tuple-element.15.refs_4_, ...), custom_call_target="tpu_custom_call" | custom-call | flops 15000000512 | bytes 1048576 | tf_op jit(solution)/shard_map/conv_sent/pallas_call | solution.py:358
  17.9 0.0 copy-start.1
  17.9 0.3 collective-permute-start.5
  18.2 1.4 %collective-permute-done.4.refs_8_ = bf16[192,768]{1,0:T(8,128)(2,1)S(1)} collective-permute-done((bf16[192,768]{1,0:T(8,128)(2,1)S(1)}, bf16[192,768]{1,0:T(8,128)(2,1)S(1)}, u32[]{:S(2)}, u32[]{:S(2)}) %collective-permute-start.4) | collective-permute-done | bytes 294944 | tf_op jit(solution)/shard_map/ppermute | solution.py:382
  19.6 4.5 %conv_own.1 = (f32[512,768]{1,0:T(8,128)S(1)}, f32[512,768]{1,0:T(8,128)S(1)}, bf16[768,768]{1,0:T(8,128)(2,1)S(1)}) custom-call(s32[1,1024]{1,0:T(1,128)S(1)} %collective-permute-done.1.refs_0_, s32[1,1024]{1,0:T(1,128)S(1)} %join.1.refs_1_, s32[1,1024]{1,0:T(1,128)S(1)} %collective-permute-done.2.refs_2_, f32[1536]{0:T(1024)S(1)} %copy-done, ...), custom_call_target="tpu_custom_call" | custom-call | flops 15000000512 | bytes 1048576 | tf_op jit(solution)/shard_map/conv_own/pallas_call | solution.py:386
  24.2 0.6 %middle.3.mine_ref = bf16[384,768]{1,0:T(8,128)(2,1)S(1)} custom-call(f32[512,768]{1,0:T(8,128)S(1)} %get-tuple-element.20.own_ref, f32[768]{0:T(1024)S(1)} %copy-done.1, bf16[192,768]{1,0:T(8,128)(2,1)S(1)} %collective-permute-done.7.refs_0_, bf16[192,768]{1,0:T(8,128)(2,1)S(1)} %collective-permute-done.8.refs_1_), custom_call_target="tpu_custom_call" | custom-call | flops 50000000 | bytes 1048576 | tf_op jit(solution)/shard_map/middle/pallas_call | solution.py:410
  24.8 5.0 %collective-permute-start.9 = (bf16[384,768]{1,0:T(8,128)(2,1)S(1)}, bf16[384,768]{1,0:T(8,128)(2,1)S(1)}, u32[]{:S(2)}, u32[]{:S(2)}) collective-permute-start(bf16[384,768]{1,0:T(8,128)(2,1)S(1)} %middle.3.mine_ref), channel_id=1, source_target_pairs={{0,1},{1,0},{2,3},{3,2},{4,5},{5,4},{6,7},{7,6},{8,9},{9,8},{10,11... | collective-permute-start | bytes 1769480 | tf_op jit(solution)/shard_map/ppermute | solution.py:419
  29.8 0.2 middle.2.mine_ref
  30.0 1.5 %collective-permute-start.6 = (bf16[128,768]{1,0:T(8,128)(2,1)S(1)}, bf16[128,768]{1,0:T(8,128)(2,1)S(1)}, u32[]{:S(2)}, u32[]{:S(2)}) collective-permute-start(bf16[128,768]{1,0:T(8,128)(2,1)S(1)} %middle.2.mine_ref), channel_id=1, source_target_pairs={{0,1},{1,0},{2,3},{3,2},{4,5},{5,4},{6,7},{7,6},{8,9},{9,8},{10,11... | collective-permute-start | bytes 589832 | tf_op jit(solution)/shard_map/ppermute | solution.py:419
  31.5 1.5 %final.2.refs_0_ = bf16[2,256,768]{2,1,0:T(8,128)(2,1)} custom-call(bf16[384,768]{1,0:T(8,128)(2,1)S(1)} %middle.3.mine_ref, bf16[384,768]{1,0:T(8,128)(2,1)S(1)} %collective-permute-done.9.other_ref, f32[512,768]{1,0:T(8,128)S(1)} %get-tuple-element.21.res_ref, bf16[768,768]{1,0:T(8,128)(2,1)S(1)} %get-tuple-element.22.point_ref), custom_call_target="tpu_custom_call" | custom-call | flops 500000000 | bytes 1048576 | tf_op jit(solution)/shard_map/final/pallas_call | solution.py:421
  33.0 1.0 %final.3 = bf16[2,256,768]{2,1,0:T(8,128)(2,1)} custom-call(bf16[128,768]{1,0:T(8,128)(2,1)S(1)} %middle.2.mine_ref, bf16[128,768]{1,0:T(8,128)(2,1)S(1)} %collective-permute-done.6.other_ref, f32[512,768]{1,0:T(8,128)S(1)} %get-tuple-element.21.res_ref, bf16[768,768]{1,0:T(8,128)(2,1)S(1)} %get-tuple-element.22.point_ref, ...), custom_call_target="tpu_custom_call", output_to_operand_aliasing={{}: (4, {})} | custom-call | flops 15000000512 | bytes 1048576 | tf_op jit(solution)/shard_map/final/pallas_call | solution.py:421
  (11 shorter events, 0.0 us)
Async XLA Ops:
  0.0 2.6 %collective-permute-start = (s32[1,512]{1,0:T(1,128)}, s32[1,512]{1,0:T(1,128)S(1)}, u32[]{:S(2)}, u32[]{:S(2)}) collective-permute-start(s32[1,512]{1,0:T(1,128)} %tok_any.1), channel_id=1, source_target_pairs={{0,2},{2,0},{1,3},{3,1},{4,6},{6,4},{5,7},{7,5},{8,10},{10,8},{9,1... | collective-permute-start | bytes 6152 | tf_op jit(solution)/shard_map/ppermute | solution.py:293
  1.2 10.3 %collective-permute-start.3 = (bf16[192,768]{1,0:T(8,128)(2,1)S(1)}, bf16[192,768]{1,0:T(8,128)(2,1)S(1)}, u32[]{:S(2)}, u32[]{:S(2)}) collective-permute-start(bf16[192,768]{1,0:T(8,128)(2,1)S(1)} %get-tuple-element.16), channel_id=1, source_target_pairs={{0,2},{2,0},{1,3},{3,1},{4,6},{6,4},{5,7},{7,5},{8,10},{10,8},{9,1... | collective-permute-start | bytes 884744 | tf_op jit(solution)/shard_map/ppermute | solution.py:335
  2.7 6.3 %copy-start = (f32[1536]{0:T(1024)S(1)}, f32[1536]{0:T(1024)}, u32[]{:S(2)}) copy-start(f32[1536]{0:T(1024)} %refs_3_.7) | copy-start | bytes 18436
  2.7 6.3 %collective-permute-start.1 = (s32[1,1024]{1,0:T(1,128)S(1)}, s32[1,1024]{1,0:T(1,128)S(1)}, u32[]{:S(2)}, u32[]{:S(2)}) collective-permute-start(s32[1,1024]{1,0:T(1,128)S(1)} %join.1.refs_1_), channel_id=1, source_target_pairs={{0,4},{8,12},{4,0},{12,8},{1,5},{9,13},{5,1},{13,9},{2,6},{10,14},... | collective-permute-start | bytes 12296 | tf_op jit(solution)/shard_map/ppermute | solution.py:317
  2.9 6.0 %collective-permute-start.2 = (s32[1,1024]{1,0:T(1,128)S(1)}, s32[1,1024]{1,0:T(1,128)S(1)}, u32[]{:S(2)}, u32[]{:S(2)}) collective-permute-start(s32[1,1024]{1,0:T(1,128)S(1)} %join.1.refs_1_), channel_id=1, source_target_pairs={{4,8},{8,4},{5,9},{9,5},{6,10},{10,6},{7,11},{11,7},{20,24},{24,20... | collective-permute-start | bytes 12296 | tf_op jit(solution)/shard_map/ppermute | solution.py:318
  11.2 13.0 %collective-permute-start.7 = (bf16[192,768]{1,0:T(8,128)(2,1)S(1)}, bf16[192,768]{1,0:T(8,128)(2,1)S(1)}, u32[]{:S(2)}, u32[]{:S(2)}) collective-permute-start(bf16[192,768]{1,0:T(8,128)(2,1)S(1)} %get-tuple-element.17.refs_6_), channel_id=1, source_target_pairs={{0,2},{2,0},{1,3},{3,1},{4,6},{6,4},{5,7},{7,5},{8,10},{10,8},{9,1... | collective-permute-start | bytes 884744 | tf_op jit(solution)/shard_map/ppermute | solution.py:375
  13.7 5.9 %collective-permute-start.4 = (bf16[192,768]{1,0:T(8,128)(2,1)S(1)}, bf16[192,768]{1,0:T(8,128)(2,1)S(1)}, u32[]{:S(2)}, u32[]{:S(2)}) collective-permute-start(bf16[192,768]{1,0:T(8,128)(2,1)S(1)} %get-tuple-element.19.refs_7_), channel_id=1, source_target_pairs={{0,16},{16,0},{1,17},{17,1},{2,18},{18,2},{3,19},{19,3},{4,20},{20... | collective-permute-start | bytes 884744 | tf_op jit(solution)/shard_map/ppermute | solution.py:382
  15.0 9.2 %collective-permute-start.8 = (bf16[192,768]{1,0:T(8,128)(2,1)S(1)}, bf16[192,768]{1,0:T(8,128)(2,1)S(1)}, u32[]{:S(2)}, u32[]{:S(2)}) collective-permute-start(bf16[192,768]{1,0:T(8,128)(2,1)S(1)} %get-tuple-element.18.refs_5_), channel_id=1, source_target_pairs={{0,2},{2,0},{1,3},{3,1},{4,6},{6,4},{5,7},{7,5},{8,10},{10,8},{9,1... | collective-permute-start | bytes 884744 | tf_op jit(solution)/shard_map/ppermute | solution.py:375
  17.9 6.3 %copy-start.1 = (f32[768]{0:T(1024)S(1)}, f32[768]{0:T(1024)}, u32[]{:S(2)}) copy-start(f32[768]{0:T(1024)} %gain_ref.3) | copy-start | bytes 9220
  17.9 11.8 %collective-permute-start.5 = (bf16[128,768]{1,0:T(8,128)(2,1)S(1)}, bf16[128,768]{1,0:T(8,128)(2,1)S(1)}, u32[]{:S(2)}, u32[]{:S(2)}) collective-permute-start(bf16[128,768]{1,0:T(8,128)(2,1)S(1)} %conv_sent.5.refs_5_), channel_id=1, source_target_pairs={{0,2},{2,0},{1,3},{3,1},{4,6},{6,4},{5,7},{7,5},{8,10},{10,8},{9,1... | collective-permute-start | bytes 589832 | tf_op jit(solution)/shard_map/ppermute | solution.py:375
  24.8 6.8 %collective-permute-start.9 = (bf16[384,768]{1,0:T(8,128)(2,1)S(1)}, bf16[384,768]{1,0:T(8,128)(2,1)S(1)}, u32[]{:S(2)}, u32[]{:S(2)}) collective-permute-start(bf16[384,768]{1,0:T(8,128)(2,1)S(1)} %middle.3.mine_ref), channel_id=1, source_target_pairs={{0,1},{1,0},{2,3},{3,2},{4,5},{5,4},{6,7},{7,6},{8,9},{9,8},{10,11... | collective-permute-start | bytes 1769480 | tf_op jit(solution)/shard_map/ppermute | solution.py:419
  30.0 3.0 %collective-permute-start.6 = (bf16[128,768]{1,0:T(8,128)(2,1)S(1)}, bf16[128,768]{1,0:T(8,128)(2,1)S(1)}, u32[]{:S(2)}, u32[]{:S(2)}) collective-permute-start(bf16[128,768]{1,0:T(8,128)(2,1)S(1)} %middle.2.mine_ref), channel_id=1, source_target_pairs={{0,1},{1,0},{2,3},{3,2},{4,5},{5,4},{6,7},{7,6},{8,9},{9,8},{10,11... | collective-permute-start | bytes 589832 | tf_op jit(solution)/shard_map/ppermute | solution.py:419

commit v2 on v1

--- a/solution.py
+++ b/solution.py
@@ -9,7 +9,7 @@
 
 DILATION = 256
 EPS = 1e-06
-ROW_STEPS = (256, 192, 64)
+ROW_STEP = 32
 CHUNKS = ((0, 96), (96, 96), (192, 64))
 TAILS = ((0, 1), (2,))
 EARLY_TAPS, LATE_TAPS = (0, 1), (2,)
@@ -81,14 +81,13 @@
     gain = jnp.broadcast_to(gain_ref[...].reshape(1, width), (8, width))
     gain = pltpu.roll(gain, turn, 1)[:1, :depth]
     tables = [pack_ref[rows] for rows in table_rows(depth, width, pack_ref.shape[1])]
-    step = next(step for step in ROW_STEPS if hot.shape[0] % step == 0)
-    for start in range(0, hot.shape[0], step):
-        rows = hot[start : start + step]
+    for start in range(0, hot.shape[0], ROW_STEP):
+        rows = hot[start : start + ROW_STEP]
         parts = [jnp.dot(rows, table, preferred_element_type=jnp.float32) for table in tables]
         square = sum(part * part for part in parts)
         mean = jnp.sum(square, axis=-1, keepdims=True) * (1.0 / width)
         scaled = parts[0][:, :depth] * lax.rsqrt(mean + EPS) * gain
-        act_ref[start : start + step] = gelu(scaled).astype(jnp.bfloat16)
+        act_ref[start : start + ROW_STEP] = gelu(scaled).astype(jnp.bfloat16)
 
 
 def convolve(act_ref, size, rows, pack_ref, copies=()):
@@ -203,16 +202,6 @@
 def rows_of(ref, low, size):
     starts = range(low, ref.shape[0], DILATION)
     return jnp.concatenate([ref[start : start + size] for start in starts])
-
-
-def middle_of(own_ref, gain_ref, parts, low, size):
-    total = rows_of(own_ref, low, size)
-    for ref in parts:
-        total = total + ref[...].astype(jnp.float32)
-    mean = jnp.mean(total * total, axis=-1, keepdims=True)
-    return gelu(total * lax.rsqrt(mean + EPS) * gain_ref[...].reshape(1, -1)).astype(
-        jnp.bfloat16
-    )
 
 
 def own_kernel(places, piece_rows, *refs):
@@ -250,13 +239,21 @@
 
 def middle_kernel(chunks, count, own_ref, gain_ref, *refs):
     out_ref = refs[-1]
+    gain = gain_ref[...].reshape(1, -1)
     first, total_size = chunks[0][0], sum(size for _, size in chunks)
     for index, (low, size) in enumerate(chunks):
         parts = refs[index * count : (index + 1) * count]
-        value = middle_of(own_ref, gain_ref, parts, low, size)
         for block in range(own_ref.shape[0] // DILATION):
-            start = block * total_size + low - first
-            out_ref[start : start + size] = value[block * size : (block + 1) * size]
+            for row in range(0, size, ROW_STEP):
+                start = block * DILATION + low + row
+                total = own_ref[start : start + ROW_STEP]
+                start = block * size + row
+                for ref in parts:
+                    total = total + ref[start : start + ROW_STEP].astype(jnp.float32)
+                mean = jnp.mean(total * total, axis=-1, keepdims=True)
+                value = gelu(total * lax.rsqrt(mean + EPS) * gain)
+                start = block * total_size + low - first + row
+                out_ref[start : start + ROW_STEP] = value.astype(jnp.bfloat16)
 
 
 def final_kernel(low, size, mine_ref, other_ref, res_ref, point_ref, *refs):

time: 34.2 us -> 33.9 us (level)
  the two profiles are of different devices: /device:TPU:11 before, /device:TPU:9 now
where the time goes in v2:
time: 33.9 us; the launch traced here: 33.7 us
  starting transfers between devices  16.2 us (48%)
  Pallas kernels  15.5 us (46%)
  waiting for transfers between devices  1.84 us (5%)
    ppermute x2, starting transfers between devices, per_device(): other = lax.ppermute(middle, 'strand', ring_pairs('strand', 1))  6.01 us
    pallas_call x3, Pallas kernels, per_device(): pl.pallas_call(functools.partial(chunk_kernel, step, low, size, row_count...  5.11 us
    ppermute x1, starting transfers between devices, per_device(): odd = lax.ppermute(joined, 'seq', pair_pairs('seq', 1))  4.48 us
    pallas_call x1, Pallas kernels, per_device(): pl.pallas_call(functools.partial(own_kernel, places, piece_rows), out_sha...  4.41 us
    ppermute x3, starting transfers between devices, per_device(): received[index].append(lax.ppermute(part, 'dp', ring_pairs('dp', step)))  2.81 us
    pallas_call x2, Pallas kernels, per_device(): pl.pallas_call(functools.partial(final_kernel, low, size), grid=(1,), out...  2.5 us
    pallas_call x1, Pallas kernels, per_device(): pl.pallas_call(load_kernel, out_shape=jax.ShapeDtypeStruct((pack_rows, in...  1.7 us
    ppermute x1, waiting for transfers between devices, per_device(): piece = lax.ppermute(piece, 'groups', ring_pairs('groups', -turn))  1.66 us
  transfers between devices with their start and end apart: 10, of which 2 were waited for; matrix products, arithmetic and copies ran while one was open for 0% of the time, Pallas kernels for 43%

profile of v2, /device:TPU:9, one launch (start us, length us, event | category | flops | bytes accessed | tf_op | source)
XLA Modules:
  0.0 33.7 jit_solution(15519792557284120189)
XLA Ops:
  0.0 1.2 %collective-permute-start = (s32[1,512]{1,0:T(1,128)}, s32[1,512]{1,0:T(1,128)S(1)}, u32[]{:S(2)}, u32[]{:S(2)}) collective-permute-start(s32[1,512]{1,0:T(1,128)} %tok_any.1), channel_id=1, source_target_pairs={{0,2},{2,0},{1,3},{3,1},{4,6},{6,4},{5,7},{7,5},{8,10},{10,8},{9,1... | collective-permute-start | bytes 6152 | tf_op jit(solution)/shard_map/ppermute | solution.py:290
  1.2 1.0 %point_slice.1 = (bf16[192,768]{1,0:T(8,128)(2,1)S(1)}, s32[1,512]{1,0:T(1,128)S(1)}) custom-call(bf16[384,1536]{1,0:T(8,128)(2,1)} %refs_6_.1, s32[1,512]{1,0:T(1,128)} %tok_any.1), custom_call_target="tpu_custom_call" | custom-call | flops 100000000 | bytes 1048576 | tf_op jit(solution)/shard_map/point_slice/pallas_call | solution.py:292
  2.2 0.3 collective-permute-start.3
  2.5 0.1 collective-permute-done.refs_1_
  2.7 0.1 collective-permute-start.1
  2.7 4.5 %collective-permute-start.2 = (s32[1,1024]{1,0:T(1,128)S(1)}, s32[1,1024]{1,0:T(1,128)S(1)}, u32[]{:S(2)}, u32[]{:S(2)}) collective-permute-start(s32[1,1024]{1,0:T(1,128)S(1)} %join.1.refs_1_), channel_id=1, source_target_pairs={{4,8},{8,4},{5,9},{9,5},{6,10},{10,6},{7,11},{11,7},{20,24},{24,20... | collective-permute-start | bytes 12296 | tf_op jit(solution)/shard_map/ppermute | solution.py:315
  7.2 1.7 %load.1.refs_4_ = bf16[2496,768]{1,0:T(8,128)(2,1)S(1)} custom-call(bf16[15,4,1536]{2,1,0:T(4,128)(2,1)} %stem_any.1, bf16[3,768,768]{2,1,0:T(8,128)(2,1)} %refs_5_.1), custom_call_target="tpu_custom_call" | custom-call | flops 100000000 | bytes 1048576 | tf_op jit(solution)/shard_map/load/pallas_call | solution.py:317
  9.0 1.9 %conv_sent.3 = (bf16[192,768]{1,0:T(8,128)(2,1)S(1)}, bf16[2496,768]{1,0:T(8,128)(2,1)S(1)}) custom-call(s32[1,1024]{1,0:T(1,128)S(1)} %collective-permute-done.1.refs_0_, s32[1,1024]{1,0:T(1,128)S(1)} %join.1.refs_1_, s32[1,1024]{1,0:T(1,128)S(1)} %collective-permute-done.2.refs_2_, f32[1536]{0:T(1024)S(1)} %copy-done, ...), custom_call_target="tpu_custom_call", output_to_operand_aliasing={{1}: (4, {})} | custom-call | flops 15000000512 | bytes 1048576 | tf_op jit(solution)/shard_map/conv_sent/pallas_call | solution.py:355
  10.9 1.3 %collective-permute-start.7 = (bf16[192,768]{1,0:T(8,128)(2,1)S(1)}, bf16[192,768]{1,0:T(8,128)(2,1)S(1)}, u32[]{:S(2)}, u32[]{:S(2)}) collective-permute-start(bf16[192,768]{1,0:T(8,128)(2,1)S(1)} %get-tuple-element.17.refs_6_), channel_id=1, source_target_pairs={{0,2},{2,0},{1,3},{3,1},{4,6},{6,4},{5,7},{7,5},{8,10},{10,8},{9,1... | collective-permute-start | bytes 884744 | tf_op jit(solution)/shard_map/ppermute | solution.py:372
  12.1 1.8 %conv_sent.4 = (bf16[192,768]{1,0:T(8,128)(2,1)S(1)}, bf16[192,768]{1,0:T(8,128)(2,1)S(1)}) custom-call(s32[1,1024]{1,0:T(1,128)S(1)} %collective-permute-done.1.refs_0_, s32[1,1024]{1,0:T(1,128)S(1)} %join.1.refs_1_, s32[1,1024]{1,0:T(1,128)S(1)} %collective-permute-done.2.refs_2_, f32[1536]{0:T(1024)S(1)} %copy-done, ...), custom_call_target="tpu_custom_call", output_to_operand_aliasing={{1}: (5, {})} | custom-call | flops 500000000 | bytes 1048576 | tf_op jit(solution)/shard_map/conv_sent/pallas_call | solution.py:355
  14.0 1.3 %collective-permute-start.4 = (bf16[192,768]{1,0:T(8,128)(2,1)S(1)}, bf16[192,768]{1,0:T(8,128)(2,1)S(1)}, u32[]{:S(2)}, u32[]{:S(2)}) collective-permute-start(bf16[192,768]{1,0:T(8,128)(2,1)S(1)} %get-tuple-element.19.refs_7_), channel_id=1, source_target_pairs={{0,16},{16,0},{1,17},{17,1},{2,18},{18,2},{3,19},{19,3},{4,20},{20... | collective-permute-start | bytes 884744 | tf_op jit(solution)/shard_map/ppermute | solution.py:379
  15.3 0.3 collective-permute-start.8
  15.5 1.4 %conv_sent.5.refs_5_ = bf16[128,768]{1,0:T(8,128)(2,1)S(1)} custom-call(s32[1,1024]{1,0:T(1,128)S(1)} %collective-permute-done.1.refs_0_, s32[1,1024]{1,0:T(1,128)S(1)} %join.1.refs_1_, s32[1,1024]{1,0:T(1,128)S(1)} %collective-permute-done.2.refs_2_, f32[1536]{0:T(1024)S(1)} %copy-done, bf16[2496,768]{1,0:T(8,128)(2,1)S(1)} %get-tuple-element.15.refs_4_, ...), custom_call_target="tpu_custom_call" | custom-call | flops 15000000512 | bytes 1048576 | tf_op jit(solution)/shard_map/conv_sent/pallas_call | solution.py:355
  16.9 0.0 copy-start.1
  16.9 1.3 %collective-permute-start.5 = (bf16[128,768]{1,0:T(8,128)(2,1)S(1)}, bf16[128,768]{1,0:T(8,128)(2,1)S(1)}, u32[]{:S(2)}, u32[]{:S(2)}) collective-permute-start(bf16[128,768]{1,0:T(8,128)(2,1)S(1)} %conv_sent.5.refs_5_), channel_id=1, source_target_pairs={{0,2},{2,0},{1,3},{3,1},{4,6},{6,4},{5,7},{7,5},{8,10},{10,8},{9,1... | collective-permute-start | bytes 589832 | tf_op jit(solution)/shard_map/ppermute | solution.py:372
  18.2 1.7 %collective-permute-done.4.refs_8_ = bf16[192,768]{1,0:T(8,128)(2,1)S(1)} collective-permute-done((bf16[192,768]{1,0:T(8,128)(2,1)S(1)}, bf16[192,768]{1,0:T(8,128)(2,1)S(1)}, u32[]{:S(2)}, u32[]{:S(2)}) %collective-permute-start.4) | collective-permute-done | bytes 294944 | tf_op jit(solution)/shard_map/ppermute | solution.py:379
  19.9 4.4 %conv_own.1 = (f32[512,768]{1,0:T(8,128)S(1)}, f32[512,768]{1,0:T(8,128)S(1)}, bf16[768,768]{1,0:T(8,128)(2,1)S(1)}) custom-call(s32[1,1024]{1,0:T(1,128)S(1)} %collective-permute-done.1.refs_0_, s32[1,1024]{1,0:T(1,128)S(1)} %join.1.refs_1_, s32[1,1024]{1,0:T(1,128)S(1)} %collective-permute-done.2.refs_2_, f32[1536]{0:T(1024)S(1)} %copy-done, ...), custom_call_target="tpu_custom_call" | custom-call | flops 15000000512 | bytes 1048576 | tf_op jit(solution)/shard_map/conv_own/pallas_call | solution.py:383
  24.3 0.0 collective-permute-done.8.refs_1_
  24.3 0.6 %middle.3.mine_ref = bf16[384,768]{1,0:T(8,128)(2,1)S(1)} custom-call(f32[512,768]{1,0:T(8,128)S(1)} %get-tuple-element.20.own_ref, f32[768]{0:T(1024)S(1)} %copy-done.1, bf16[192,768]{1,0:T(8,128)(2,1)S(1)} %collective-permute-done.7.refs_0_, bf16[192,768]{1,0:T(8,128)(2,1)S(1)} %collective-permute-done.8.refs_1_), custom_call_target="tpu_custom_call" | custom-call | flops 50000000 | bytes 1048576 | tf_op jit(solution)/shard_map/middle/pallas_call | solution.py:407
  24.9 4.3 %collective-permute-start.9 = (bf16[384,768]{1,0:T(8,128)(2,1)S(1)}, bf16[384,768]{1,0:T(8,128)(2,1)S(1)}, u32[]{:S(2)}, u32[]{:S(2)}) collective-permute-start(bf16[384,768]{1,0:T(8,128)(2,1)S(1)} %middle.3.mine_ref), channel_id=1, source_target_pairs={{0,1},{1,0},{2,3},{3,2},{4,5},{5,4},{6,7},{7,6},{8,9},{9,8},{10,11... | collective-permute-start | bytes 1769480 | tf_op jit(solution)/shard_map/ppermute | solution.py:416
  29.3 0.2 middle.2.mine_ref
  29.5 1.7 %collective-permute-start.6 = (bf16[128,768]{1,0:T(8,128)(2,1)S(1)}, bf16[128,768]{1,0:T(8,128)(2,1)S(1)}, u32[]{:S(2)}, u32[]{:S(2)}) collective-permute-start(bf16[128,768]{1,0:T(8,128)(2,1)S(1)} %middle.2.mine_ref), channel_id=1, source_target_pairs={{0,1},{1,0},{2,3},{3,2},{4,5},{5,4},{6,7},{7,6},{8,9},{9,8},{10,11... | collective-permute-start | bytes 589832 | tf_op jit(solution)/shard_map/ppermute | solution.py:416
  31.2 1.5 %final.2.refs_0_ = bf16[2,256,768]{2,1,0:T(8,128)(2,1)} custom-call(bf16[384,768]{1,0:T(8,128)(2,1)S(1)} %middle.3.mine_ref, bf16[384,768]{1,0:T(8,128)(2,1)S(1)} %collective-permute-done.9.other_ref, f32[512,768]{1,0:T(8,128)S(1)} %get-tuple-element.21.res_ref, bf16[768,768]{1,0:T(8,128)(2,1)S(1)} %get-tuple-element.22.point_ref), custom_call_target="tpu_custom_call" | custom-call | flops 500000000 | bytes 1048576 | tf_op jit(solution)/shard_map/final/pallas_call | solution.py:418
  32.7 1.0 %final.3 = bf16[2,256,768]{2,1,0:T(8,128)(2,1)} custom-call(bf16[128,768]{1,0:T(8,128)(2,1)S(1)} %middle.2.mine_ref, bf16[128,768]{1,0:T(8,128)(2,1)S(1)} %collective-permute-done.6.other_ref, f32[512,768]{1,0:T(8,128)S(1)} %get-tuple-element.21.res_ref, bf16[768,768]{1,0:T(8,128)(2,1)S(1)} %get-tuple-element.22.point_ref, ...), custom_call_target="tpu_custom_call", output_to_operand_aliasing={{}: (4, {})} | custom-call | flops 15000000512 | bytes 1048576 | tf_op jit(solution)/shard_map/final/pallas_call | solution.py:418
  (11 shorter events, 0.0 us)
Async XLA Ops:
  0.0 2.6 %collective-permute-start = (s32[1,512]{1,0:T(1,128)}, s32[1,512]{1,0:T(1,128)S(1)}, u32[]{:S(2)}, u32[]{:S(2)}) collective-permute-start(s32[1,512]{1,0:T(1,128)} %tok_any.1), channel_id=1, source_target_pairs={{0,2},{2,0},{1,3},{3,1},{4,6},{6,4},{5,7},{7,5},{8,10},{10,8},{9,1... | collective-permute-start | bytes 6152 | tf_op jit(solution)/shard_map/ppermute | solution.py:290
  2.2 9.9 %collective-permute-start.3 = (bf16[192,768]{1,0:T(8,128)(2,1)S(1)}, bf16[192,768]{1,0:T(8,128)(2,1)S(1)}, u32[]{:S(2)}, u32[]{:S(2)}) collective-permute-start(bf16[192,768]{1,0:T(8,128)(2,1)S(1)} %get-tuple-element.16), channel_id=1, source_target_pairs={{0,2},{2,0},{1,3},{3,1},{4,6},{6,4},{5,7},{7,5},{8,10},{10,8},{9,1... | collective-permute-start | bytes 884744 | tf_op jit(solution)/shard_map/ppermute | solution.py:332
  2.7 6.3 %copy-start = (f32[1536]{0:T(1024)S(1)}, f32[1536]{0:T(1024)}, u32[]{:S(2)}) copy-start(f32[1536]{0:T(1024)} %refs_3_.7) | copy-start | bytes 18436
  2.7 6.3 %collective-permute-start.1 = (s32[1,1024]{1,0:T(1,128)S(1)}, s32[1,1024]{1,0:T(1,128)S(1)}, u32[]{:S(2)}, u32[]{:S(2)}) collective-permute-start(s32[1,1024]{1,0:T(1,128)S(1)} %join.1.refs_1_), channel_id=1, source_target_pairs={{0,4},{8,12},{4,0},{12,8},{1,5},{9,13},{5,1},{13,9},{2,6},{10,14},... | collective-permute-start | bytes 12296 | tf_op jit(solution)/shard_map/ppermute | solution.py:314
  2.7 6.2 %collective-permute-start.2 = (s32[1,1024]{1,0:T(1,128)S(1)}, s32[1,1024]{1,0:T(1,128)S(1)}, u32[]{:S(2)}, u32[]{:S(2)}) collective-permute-start(s32[1,1024]{1,0:T(1,128)S(1)} %join.1.refs_1_), channel_id=1, source_target_pairs={{4,8},{8,4},{5,9},{9,5},{6,10},{10,6},{7,11},{11,7},{20,24},{24,20... | collective-permute-start | bytes 12296 | tf_op jit(solution)/shard_map/ppermute | solution.py:315
  10.9 13.4 %collective-permute-start.7 = (bf16[192,768]{1,0:T(8,128)(2,1)S(1)}, bf16[192,768]{1,0:T(8,128)(2,1)S(1)}, u32[]{:S(2)}, u32[]{:S(2)}) collective-permute-start(bf16[192,768]{1,0:T(8,128)(2,1)S(1)} %get-tuple-element.17.refs_6_), channel_id=1, source_target_pairs={{0,2},{2,0},{1,3},{3,1},{4,6},{6,4},{5,7},{7,5},{8,10},{10,8},{9,1... | collective-permute-start | bytes 884744 | tf_op jit(solution)/shard_map/ppermute | solution.py:372
  14.0 5.9 %collective-permute-start.4 = (bf16[192,768]{1,0:T(8,128)(2,1)S(1)}, bf16[192,768]{1,0:T(8,128)(2,1)S(1)}, u32[]{:S(2)}, u32[]{:S(2)}) collective-permute-start(bf16[192,768]{1,0:T(8,128)(2,1)S(1)} %get-tuple-element.19.refs_7_), channel_id=1, source_target_pairs={{0,16},{16,0},{1,17},{17,1},{2,18},{18,2},{3,19},{19,3},{4,20},{20... | collective-permute-start | bytes 884744 | tf_op jit(solution)/shard_map/ppermute | solution.py:379
  15.3 9.1 %collective-permute-start.8 = (bf16[192,768]{1,0:T(8,128)(2,1)S(1)}, bf16[192,768]{1,0:T(8,128)(2,1)S(1)}, u32[]{:S(2)}, u32[]{:S(2)}) collective-permute-start(bf16[192,768]{1,0:T(8,128)(2,1)S(1)} %get-tuple-element.18.refs_5_), channel_id=1, source_target_pairs={{0,2},{2,0},{1,3},{3,1},{4,6},{6,4},{5,7},{7,5},{8,10},{10,8},{9,1... | collective-permute-start | bytes 884744 | tf_op jit(solution)/shard_map/ppermute | solution.py:372
  16.9 7.4 %copy-start.1 = (f32[768]{0:T(1024)S(1)}, f32[768]{0:T(1024)}, u32[]{:S(2)}) copy-start(f32[768]{0:T(1024)} %gain_ref.3) | copy-start | bytes 9220
  16.9 12.3 %collective-permute-start.5 = (bf16[128,768]{1,0:T(8,128)(2,1)S(1)}, bf16[128,768]{1,0:T(8,128)(2,1)S(1)}, u32[]{:S(2)}, u32[]{:S(2)}) collective-permute-start(bf16[128,768]{1,0:T(8,128)(2,1)S(1)} %conv_sent.5.refs_5_), channel_id=1, source_target_pairs={{0,2},{2,0},{1,3},{3,1},{4,6},{6,4},{5,7},{7,5},{8,10},{10,8},{9,1... | collective-permute-start | bytes 589832 | tf_op jit(solution)/shard_map/ppermute | solution.py:372
  24.9 6.3 %collective-permute-start.9 = (bf16[384,768]{1,0:T(8,128)(2,1)S(1)}, bf16[384,768]{1,0:T(8,128)(2,1)S(1)}, u32[]{:S(2)}, u32[]{:S(2)}) collective-permute-start(bf16[384,768]{1,0:T(8,128)(2,1)S(1)} %middle.3.mine_ref), channel_id=1, source_target_pairs={{0,1},{1,0},{2,3},{3,2},{4,5},{5,4},{6,7},{7,6},{8,9},{9,8},{10,11... | collective-permute-start | bytes 1769480 | tf_op jit(solution)/shard_map/ppermute | solution.py:416
  29.5 3.2 %collective-permute-start.6 = (bf16[128,768]{1,0:T(8,128)(2,1)S(1)}, bf16[128,768]{1,0:T(8,128)(2,1)S(1)}, u32[]{:S(2)}, u32[]{:S(2)}) collective-permute-start(bf16[128,768]{1,0:T(8,128)(2,1)S(1)} %middle.2.mine_ref), channel_id=1, source_target_pairs={{0,1},{1,0},{2,3},{3,2},{4,5},{5,4},{6,7},{7,6},{8,9},{9,8},{10,11... | collective-permute-start | bytes 589832 | tf_op jit(solution)/shard_map/ppermute | solution.py:416

commit v3 on v2

--- a/solution.py
+++ b/solution.py
@@ -10,7 +10,7 @@
 DILATION = 256
 EPS = 1e-06
 ROW_STEP = 32
-CHUNKS = ((0, 96), (96, 96), (192, 64))
+CHUNKS = ((0, 64), (64, 128), (192, 64))
 TAILS = ((0, 1), (2,))
 EARLY_TAPS, LATE_TAPS = (0, 1), (2,)
 KINDS = 4
@@ -44,7 +44,7 @@
 def base_taps(sides, step, row_count):
     blocks, here = lax.axis_size("seq"), lax.axis_index("seq")
     low = step * row_count
-    even, middle, odd = [ref[:, low : low + row_count] for ref in sides]
+    odd, middle, even = [ref[:, low : low + row_count] for ref in sides]
     second = lax.rem(here, 2) == 1
     below, above = jnp.where(second, even, odd), jnp.where(second, odd, even)
     bases = jnp.concatenate([below, middle, above], axis=1)
@@ -311,8 +311,8 @@
         cost_estimate=cost("early"),
         name="join",
     )(here, *others)
+    odd = lax.ppermute(joined, "seq", pair_pairs("seq", 1))
     even = lax.ppermute(joined, "seq", pair_pairs("seq", 0))
-    odd = lax.ppermute(joined, "seq", pair_pairs("seq", 1))
     pack_rows = 3 * depth + (width // inner + 1) * TABLE
     pack = pl.pallas_call(
         load_kernel,
@@ -336,7 +336,7 @@
         for index, (low, size) in enumerate(CHUNKS):
             rows = row_count // DILATION * size
             loading, passing = step == 1 and index == 0, index == 1
-            operands = [even, joined, odd, gain_in, pack]
+            operands = [odd, joined, even, gain_in, pack]
             shapes = [jax.ShapeDtypeStruct((rows, inner), bf16)]
             scratch = [pltpu.VMEM((rows + 2 * size, depth), bf16)]
             aliases = {}
@@ -396,7 +396,7 @@
         compiler_params=params,
         cost_estimate=cost("own"),
         name="conv_own",
-    )(even, joined, odd, gain_in, pack, part, *pieces)
+    )(odd, joined, even, gain_in, pack, part, *pieces)
 
     out = None
     blocks = row_count // DILATION

time: 33.9 us -> 35.4 us (1.044)
  the two profiles are of different devices: /device:TPU:9 before, /device:TPU:0 now
where the time goes in v3:
time: 35.4 us; the launch traced here: 35.2 us
  Pallas kernels  15.7 us (44%)
  starting transfers between devices  14.1 us (40%)
  waiting for transfers between devices  5.35 us (15%)
    pallas_call x3, Pallas kernels, per_device(): pl.pallas_call(functools.partial(chunk_kernel, step, low, size, row_count...  5.28 us
    ppermute x1, starting transfers between devices, per_device(): even = lax.ppermute(joined, 'seq', pair_pairs('seq', 0))  5 us
    pallas_call x1, Pallas kernels, per_device(): pl.pallas_call(functools.partial(own_kernel, places, piece_rows), out_sha...  4.38 us
    ppermute x3, starting transfers between devices, per_device(): received[index].append(lax.ppermute(part, 'dp', ring_pairs('dp', step)))  3.67 us
    ppermute x1, starting transfers between devices, per_device(): lax.ppermute(tokens, 'dp', ring_pairs('dp', -step))  2.94 us
    ppermute x3, waiting for transfers between devices, per_device(): received[index].append(lax.ppermute(part, 'dp', ring_pairs('dp', step)))  2.71 us
    pallas_call x2, Pallas kernels, per_device(): pl.pallas_call(functools.partial(final_kernel, low, size), grid=(1,), out...  2.49 us
    ppermute x1, waiting for transfers between devices, per_device(): piece = lax.ppermute(piece, 'groups', ring_pairs('groups', -turn))  1.7 us
  transfers between devices with their start and end apart: 10, of which 5 were waited for; matrix products, arithmetic and copies ran while one was open for 0% of the time, Pallas kernels for 42%

profile of v3, /device:TPU:0, one launch (start us, length us, event | category | flops | bytes accessed | tf_op | source)
XLA Modules:
  0.0 35.2 jit_solution(6528653614584278021)
XLA Ops:
  0.0 2.9 %collective-permute-start = (s32[1,512]{1,0:T(1,128)}, s32[1,512]{1,0:T(1,128)S(1)}, u32[]{:S(2)}, u32[]{:S(2)}) collective-permute-start(s32[1,512]{1,0:T(1,128)} %tok_any.1), channel_id=1, source_target_pairs={{0,2},{2,0},{1,3},{3,1},{4,6},{6,4},{5,7},{7,5},{8,10},{10,8},{9,1... | collective-permute-start | bytes 6152 | tf_op jit(solution)/shard_map/ppermute | solution.py:290
  2.9 1.0 %point_slice.1 = (bf16[192,768]{1,0:T(8,128)(2,1)S(1)}, s32[1,512]{1,0:T(1,128)S(1)}) custom-call(bf16[384,1536]{1,0:T(8,128)(2,1)} %refs_6_.1, s32[1,512]{1,0:T(1,128)} %tok_any.1), custom_call_target="tpu_custom_call" | custom-call | flops 100000000 | bytes 1048576 | tf_op jit(solution)/shard_map/point_slice/pallas_call | solution.py:292
  4.0 0.7 %collective-permute-done.refs_1_ = s32[1,512]{1,0:T(1,128)S(1)} collective-permute-done((s32[1,512]{1,0:T(1,128)}, s32[1,512]{1,0:T(1,128)S(1)}, u32[]{:S(2)}, u32[]{:S(2)}) %collective-permute-start) | collective-permute-done | bytes 2080 | tf_op jit(solution)/shard_map/ppermute | solution.py:290
  4.7 0.7 %collective-permute-start.1 = (s32[1,1024]{1,0:T(1,128)S(1)}, s32[1,1024]{1,0:T(1,128)S(1)}, u32[]{:S(2)}, u32[]{:S(2)}) collective-permute-start(s32[1,1024]{1,0:T(1,128)S(1)} %join.1.refs_1_), channel_id=1, source_target_pairs={{4,8},{8,4},{5,9},{9,5},{6,10},{10,6},{7,11},{11,7},{20,24},{24,20... | collective-permute-start | bytes 12296 | tf_op jit(solution)/shard_map/ppermute | solution.py:314
  5.4 5.0 %collective-permute-start.2 = (s32[1,1024]{1,0:T(1,128)S(1)}, s32[1,1024]{1,0:T(1,128)S(1)}, u32[]{:S(2)}, u32[]{:S(2)}) collective-permute-start(s32[1,1024]{1,0:T(1,128)S(1)} %join.1.refs_1_), channel_id=1, source_target_pairs={{0,4},{8,12},{4,0},{12,8},{1,5},{9,13},{5,1},{13,9},{2,6},{10,14},... | collective-permute-start | bytes 12296 | tf_op jit(solution)/shard_map/ppermute | solution.py:315
  10.4 1.7 %load.1.refs_4_ = bf16[2496,768]{1,0:T(8,128)(2,1)S(1)} custom-call(bf16[15,4,1536]{2,1,0:T(4,128)(2,1)} %stem_any.1, bf16[3,768,768]{2,1,0:T(8,128)(2,1)} %refs_5_.1), custom_call_target="tpu_custom_call" | custom-call | flops 100000000 | bytes 1048576 | tf_op jit(solution)/shard_map/load/pallas_call | solution.py:317
  12.1 1.7 %conv_sent.3 = (bf16[128,768]{1,0:T(8,128)(2,1)S(1)}, bf16[2496,768]{1,0:T(8,128)(2,1)S(1)}) custom-call(s32[1,1024]{1,0:T(1,128)S(1)} %collective-permute-done.1.refs_0_, s32[1,1024]{1,0:T(1,128)S(1)} %join.1.refs_1_, s32[1,1024]{1,0:T(1,128)S(1)} %collective-permute-done.2.refs_2_, f32[1536]{0:T(1024)S(1)} %copy-done, ...), custom_call_target="tpu_custom_call", output_to_operand_aliasing={{1}: (4, {})} | custom-call | flops 15000000512 | bytes 1048576 | tf_op jit(solution)/shard_map/conv_sent/pallas_call | solution.py:355
  13.8 1.6 %collective-permute-start.7 = (bf16[128,768]{1,0:T(8,128)(2,1)S(1)}, bf16[128,768]{1,0:T(8,128)(2,1)S(1)}, u32[]{:S(2)}, u32[]{:S(2)}) collective-permute-start(bf16[128,768]{1,0:T(8,128)(2,1)S(1)} %get-tuple-element.17.refs_6_), channel_id=1, source_target_pairs={{0,2},{2,0},{1,3},{3,1},{4,6},{6,4},{5,7},{7,5},{8,10},{10,8},{9,1... | collective-permute-start | bytes 589832 | tf_op jit(solution)/shard_map/ppermute | solution.py:372
  15.4 2.2 %conv_sent.4 = (bf16[256,768]{1,0:T(8,128)(2,1)S(1)}, bf16[192,768]{1,0:T(8,128)(2,1)S(1)}) custom-call(s32[1,1024]{1,0:T(1,128)S(1)} %collective-permute-done.1.refs_0_, s32[1,1024]{1,0:T(1,128)S(1)} %join.1.refs_1_, s32[1,1024]{1,0:T(1,128)S(1)} %collective-permute-done.2.refs_2_, f32[1536]{0:T(1024)S(1)} %copy-done, ...), custom_call_target="tpu_custom_call", output_to_operand_aliasing={{1}: (5, {})} | custom-call | flops 500000000 | bytes 1048576 | tf_op jit(solution)/shard_map/conv_sent/pallas_call | solution.py:355
  17.6 1.6 %collective-permute-start.4 = (bf16[192,768]{1,0:T(8,128)(2,1)S(1)}, bf16[192,768]{1,0:T(8,128)(2,1)S(1)}, u32[]{:S(2)}, u32[]{:S(2)}) collective-permute-start(bf16[192,768]{1,0:T(8,128)(2,1)S(1)} %get-tuple-element.19.refs_7_), channel_id=1, source_target_pairs={{0,16},{16,0},{1,17},{17,1},{2,18},{18,2},{3,19},{19,3},{4,20},{20... | collective-permute-start | bytes 884744 | tf_op jit(solution)/shard_map/ppermute | solution.py:379
  19.2 0.5 %collective-permute-start.8 = (bf16[256,768]{1,0:T(8,128)(2,1)S(1)}, bf16[256,768]{1,0:T(8,128)(2,1)S(1)}, u32[]{:S(2)}, u32[]{:S(2)}) collective-permute-start(bf16[256,768]{1,0:T(8,128)(2,1)S(1)} %get-tuple-element.18.refs_5_), channel_id=1, source_target_pairs={{0,2},{2,0},{1,3},{3,1},{4,6},{6,4},{5,7},{7,5},{8,10},{10,8},{9,1... | collective-permute-start | bytes 1179656 | tf_op jit(solution)/shard_map/ppermute | solution.py:372
  19.7 1.4 %conv_sent.5.refs_5_ = bf16[128,768]{1,0:T(8,128)(2,1)S(1)} custom-call(s32[1,1024]{1,0:T(1,128)S(1)} %collective-permute-done.1.refs_0_, s32[1,1024]{1,0:T(1,128)S(1)} %join.1.refs_1_, s32[1,1024]{1,0:T(1,128)S(1)} %collective-permute-done.2.refs_2_, f32[1536]{0:T(1024)S(1)} %copy-done, bf16[2496,768]{1,0:T(8,128)(2,1)S(1)} %get-tuple-element.15.refs_4_, ...), custom_call_target="tpu_custom_call" | custom-call | flops 15000000512 | bytes 1048576 | tf_op jit(solution)/shard_map/conv_sent/pallas_call | solution.py:355
  21.1 1.6 %collective-permute-start.5 = (bf16[128,768]{1,0:T(8,128)(2,1)S(1)}, bf16[128,768]{1,0:T(8,128)(2,1)S(1)}, u32[]{:S(2)}, u32[]{:S(2)}) collective-permute-start(bf16[128,768]{1,0:T(8,128)(2,1)S(1)} %conv_sent.5.refs_5_), channel_id=1, source_target_pairs={{0,2},{2,0},{1,3},{3,1},{4,6},{6,4},{5,7},{7,5},{8,10},{10,8},{9,1... | collective-permute-start | bytes 589832 | tf_op jit(solution)/shard_map/ppermute | solution.py:372
  22.7 1.7 %collective-permute-done.4.refs_8_ = bf16[192,768]{1,0:T(8,128)(2,1)S(1)} collective-permute-done((bf16[192,768]{1,0:T(8,128)(2,1)S(1)}, bf16[192,768]{1,0:T(8,128)(2,1)S(1)}, u32[]{:S(2)}, u32[]{:S(2)}) %collective-permute-start.4) | collective-permute-done | bytes 294944 | tf_op jit(solution)/shard_map/ppermute | solution.py:379
  24.4 4.4 %conv_own.1 = (f32[512,768]{1,0:T(8,128)S(1)}, f32[512,768]{1,0:T(8,128)S(1)}, bf16[768,768]{1,0:T(8,128)(2,1)S(1)}) custom-call(s32[1,1024]{1,0:T(1,128)S(1)} %collective-permute-done.1.refs_0_, s32[1,1024]{1,0:T(1,128)S(1)} %join.1.refs_1_, s32[1,1024]{1,0:T(1,128)S(1)} %collective-permute-done.2.refs_2_, f32[1536]{0:T(1024)S(1)} %copy-done, ...), custom_call_target="tpu_custom_call" | custom-call | flops 15000000512 | bytes 1048576 | tf_op jit(solution)/shard_map/conv_own/pallas_call | solution.py:383
  28.8 1.3 %collective-permute-done.8.refs_1_ = bf16[256,768]{1,0:T(8,128)(2,1)S(1)} collective-permute-done((bf16[256,768]{1,0:T(8,128)(2,1)S(1)}, bf16[256,768]{1,0:T(8,128)(2,1)S(1)}, u32[]{:S(2)}, u32[]{:S(2)}) %collective-permute-start.8) | collective-permute-done | bytes 393248 | tf_op jit(solution)/shard_map/ppermute | solution.py:372
  30.1 0.6 %middle.3.mine_ref = bf16[384,768]{1,0:T(8,128)(2,1)S(1)} custom-call(f32[512,768]{1,0:T(8,128)S(1)} %get-tuple-element.20.own_ref, f32[768]{0:T(1024)S(1)} %copy-done.1, bf16[128,768]{1,0:T(8,128)(2,1)S(1)} %collective-permute-done.7.refs_0_, bf16[256,768]{1,0:T(8,128)(2,1)S(1)} %collective-permute-done.8.refs_1_), custom_call_target="tpu_custom_call" | custom-call | flops 50000000 | bytes 1048576 | tf_op jit(solution)/shard_map/middle/pallas_call | solution.py:407
  30.7 0.1 collective-permute-start.9
  30.7 1.4 %collective-permute-done.5.refs_0_ = bf16[128,768]{1,0:T(8,128)(2,1)S(1)} collective-permute-done((bf16[128,768]{1,0:T(8,128)(2,1)S(1)}, bf16[128,768]{1,0:T(8,128)(2,1)S(1)}, u32[]{:S(2)}, u32[]{:S(2)}) %collective-permute-start.5) | collective-permute-done | bytes 196640 | tf_op jit(solution)/shard_map/ppermute | solution.py:372
  32.2 0.2 middle.2.mine_ref
  32.4 0.1 collective-permute-start.6
  32.5 0.2 collective-permute-done.9.other_ref
  32.7 1.5 %final.2.refs_0_ = bf16[2,256,768]{2,1,0:T(8,128)(2,1)} custom-call(bf16[384,768]{1,0:T(8,128)(2,1)S(1)} %middle.3.mine_ref, bf16[384,768]{1,0:T(8,128)(2,1)S(1)} %collective-permute-done.9.other_ref, f32[512,768]{1,0:T(8,128)S(1)} %get-tuple-element.21.res_ref, bf16[768,768]{1,0:T(8,128)(2,1)S(1)} %get-tuple-element.22.point_ref), custom_call_target="tpu_custom_call" | custom-call | flops 500000000 | bytes 1048576 | tf_op jit(solution)/shard_map/final/pallas_call | solution.py:418
  34.2 1.0 %final.3 = bf16[2,256,768]{2,1,0:T(8,128)(2,1)} custom-call(bf16[128,768]{1,0:T(8,128)(2,1)S(1)} %middle.2.mine_ref, bf16[128,768]{1,0:T(8,128)(2,1)S(1)} %collective-permute-done.6.other_ref, f32[512,768]{1,0:T(8,128)S(1)} %get-tuple-element.21.res_ref, bf16[768,768]{1,0:T(8,128)(2,1)S(1)} %get-tuple-element.22.point_ref, ...), custom_call_target="tpu_custom_call", output_to_operand_aliasing={{}: (4, {})} | custom-call | flops 15000000512 | bytes 1048576 | tf_op jit(solution)/shard_map/final/pallas_call | solution.py:418
  (11 shorter events, 0.1 us)
Async XLA Ops:
  0.0 4.7 %collective-permute-start = (s32[1,512]{1,0:T(1,128)}, s32[1,512]{1,0:T(1,128)S(1)}, u32[]{:S(2)}, u32[]{:S(2)}) collective-permute-start(s32[1,512]{1,0:T(1,128)} %tok_any.1), channel_id=1, source_target_pairs={{0,2},{2,0},{1,3},{3,1},{4,6},{6,4},{5,7},{7,5},{8,10},{10,8},{9,1... | collective-permute-start | bytes 6152 | tf_op jit(solution)/shard_map/ppermute | solution.py:290
  3.9 11.4 %collective-permute-start.3 = (bf16[192,768]{1,0:T(8,128)(2,1)S(1)}, bf16[192,768]{1,0:T(8,128)(2,1)S(1)}, u32[]{:S(2)}, u32[]{:S(2)}) collective-permute-start(bf16[192,768]{1,0:T(8,128)(2,1)S(1)} %get-tuple-element.16), channel_id=1, source_target_pairs={{0,2},{2,0},{1,3},{3,1},{4,6},{6,4},{5,7},{7,5},{8,10},{10,8},{9,1... | collective-permute-start | bytes 884744 | tf_op jit(solution)/shard_map/ppermute | solution.py:332
  4.7 7.4 %copy-start = (f32[1536]{0:T(1024)S(1)}, f32[1536]{0:T(1024)}, u32[]{:S(2)}) copy-start(f32[1536]{0:T(1024)} %refs_3_.7) | copy-start | bytes 18436
  4.7 7.4 %collective-permute-start.1 = (s32[1,1024]{1,0:T(1,128)S(1)}, s32[1,1024]{1,0:T(1,128)S(1)}, u32[]{:S(2)}, u32[]{:S(2)}) collective-permute-start(s32[1,1024]{1,0:T(1,128)S(1)} %join.1.refs_1_), channel_id=1, source_target_pairs={{4,8},{8,4},{5,9},{9,5},{6,10},{10,6},{7,11},{11,7},{20,24},{24,20... | collective-permute-start | bytes 12296 | tf_op jit(solution)/shard_map/ppermute | solution.py:314
  5.4 6.7 %collective-permute-start.2 = (s32[1,1024]{1,0:T(1,128)S(1)}, s32[1,1024]{1,0:T(1,128)S(1)}, u32[]{:S(2)}, u32[]{:S(2)}) collective-permute-start(s32[1,1024]{1,0:T(1,128)S(1)} %join.1.refs_1_), channel_id=1, source_target_pairs={{0,4},{8,12},{4,0},{12,8},{1,5},{9,13},{5,1},{13,9},{2,6},{10,14},... | collective-permute-start | bytes 12296 | tf_op jit(solution)/shard_map/ppermute | solution.py:315
  13.8 15.0 %collective-permute-start.7 = (bf16[128,768]{1,0:T(8,128)(2,1)S(1)}, bf16[128,768]{1,0:T(8,128)(2,1)S(1)}, u32[]{:S(2)}, u32[]{:S(2)}) collective-permute-start(bf16[128,768]{1,0:T(8,128)(2,1)S(1)} %get-tuple-element.17.refs_6_), channel_id=1, source_target_pairs={{0,2},{2,0},{1,3},{3,1},{4,6},{6,4},{5,7},{7,5},{8,10},{10,8},{9,1... | collective-permute-start | bytes 589832 | tf_op jit(solution)/shard_map/ppermute | solution.py:372
  17.6 6.8 %collective-permute-start.4 = (bf16[192,768]{1,0:T(8,128)(2,1)S(1)}, bf16[192,768]{1,0:T(8,128)(2,1)S(1)}, u32[]{:S(2)}, u32[]{:S(2)}) collective-permute-start(bf16[192,768]{1,0:T(8,128)(2,1)S(1)} %get-tuple-element.19.refs_7_), channel_id=1, source_target_pairs={{0,16},{16,0},{1,17},{17,1},{2,18},{18,2},{3,19},{19,3},{4,20},{20... | collective-permute-start | bytes 884744 | tf_op jit(solution)/shard_map/ppermute | solution.py:379
  19.2 10.9 %collective-permute-start.8 = (bf16[256,768]{1,0:T(8,128)(2,1)S(1)}, bf16[256,768]{1,0:T(8,128)(2,1)S(1)}, u32[]{:S(2)}, u32[]{:S(2)}) collective-permute-start(bf16[256,768]{1,0:T(8,128)(2,1)S(1)} %get-tuple-element.18.refs_5_), channel_id=1, source_target_pairs={{0,2},{2,0},{1,3},{3,1},{4,6},{6,4},{5,7},{7,5},{8,10},{10,8},{9,1... | collective-permute-start | bytes 1179656 | tf_op jit(solution)/shard_map/ppermute | solution.py:372
  21.1 9.0 %copy-start.1 = (f32[768]{0:T(1024)S(1)}, f32[768]{0:T(1024)}, u32[]{:S(2)}) copy-start(f32[768]{0:T(1024)} %gain_ref.3) | copy-start | bytes 9220
  21.1 11.1 %collective-permute-start.5 = (bf16[128,768]{1,0:T(8,128)(2,1)S(1)}, bf16[128,768]{1,0:T(8,128)(2,1)S(1)}, u32[]{:S(2)}, u32[]{:S(2)}) collective-permute-start(bf16[128,768]{1,0:T(8,128)(2,1)S(1)} %conv_sent.5.refs_5_), channel_id=1, source_target_pairs={{0,2},{2,0},{1,3},{3,1},{4,6},{6,4},{5,7},{7,5},{8,10},{10,8},{9,1... | collective-permute-start | bytes 589832 | tf_op jit(solution)/shard_map/ppermute | solution.py:372
  30.7 2.1 %collective-permute-start.9 = (bf16[384,768]{1,0:T(8,128)(2,1)S(1)}, bf16[384,768]{1,0:T(8,128)(2,1)S(1)}, u32[]{:S(2)}, u32[]{:S(2)}) collective-permute-start(bf16[384,768]{1,0:T(8,128)(2,1)S(1)} %middle.3.mine_ref), channel_id=1, source_target_pairs={{0,1},{1,0},{2,3},{3,2},{4,5},{5,4},{6,7},{7,6},{8,9},{9,8},{10,11... | collective-permute-start | bytes 1769480 | tf_op jit(solution)/shard_map/ppermute | solution.py:416
  32.4 1.8 %collective-permute-start.6 = (bf16[128,768]{1,0:T(8,128)(2,1)S(1)}, bf16[128,768]{1,0:T(8,128)(2,1)S(1)}, u32[]{:S(2)}, u32[]{:S(2)}) collective-permute-start(bf16[128,768]{1,0:T(8,128)(2,1)S(1)} %middle.2.mine_ref), channel_id=1, source_target_pairs={{0,1},{1,0},{2,3},{3,2},{4,5},{5,4},{6,7},{7,6},{8,9},{9,8},{10,11... | collective-permute-start | bytes 589832 | tf_op jit(solution)/shard_map/ppermute | solution.py:416

commit v4 on v2

--- a/solution.py
+++ b/solution.py
@@ -11,21 +11,23 @@
 EPS = 1e-06
 ROW_STEP = 32
 CHUNKS = ((0, 96), (96, 96), (192, 64))
-TAILS = ((0, 1), (2,))
+TAILS = ((0,), (1,), (2,))
 EARLY_TAPS, LATE_TAPS = (0, 1), (2,)
 KINDS = 4
 TABLE = 16 * KINDS
-FLOPS = {
+WEIGHTS = {
     "early": 0.1,
     "load": 0.1,
     "sent0": 15.0,
     "sent1": 0.5,
-    "sent2": 15.0,
+    "sent2": 5.0,
     "own": 15.0,
     "middle0": 0.05,
     "middle1": 5.0,
-    "final0": 0.5,
-    "final1": 15.0,
+    "middle2": 5.0,
+    "final0": 0.05,
+    "final1": 0.5,
+    "final2": 15.0,
 }
 MIB = 2**20
 
@@ -256,8 +258,9 @@
                 out_ref[start : start + ROW_STEP] = value.astype(jnp.bfloat16)
 
 
-def final_kernel(low, size, mine_ref, other_ref, res_ref, point_ref, *refs):
-    out_ref = refs[-1]
+def final_kernel(low, size, out_index, mine_ref, other_ref, res_ref, point_ref, *refs):
+    out_ref, tick_ref = refs[out_index - 4 :]
+    tick_ref[...] = jnp.zeros_like(tick_ref)
     total = mine_ref[...].astype(jnp.float32) + other_ref[...].astype(jnp.float32)
     branch = jnp.dot(
         total.astype(jnp.bfloat16), point_ref[...], preferred_element_type=jnp.float32
@@ -272,7 +275,7 @@
 
 def cost(kind):
     return pl.CostEstimate(
-        flops=int(1e9 * FLOPS[kind]), bytes_accessed=2**20, transcendentals=0
+        flops=int(1e9 * WEIGHTS[kind]), bytes_accessed=2**20, transcendentals=0
     )
 
 
@@ -398,34 +401,42 @@
         name="conv_own",
     )(even, joined, odd, gain_in, pack, part, *pieces)
 
-    out = None
+    out, ticks = None, []
     blocks = row_count // DILATION
     for index, tail in enumerate(TAILS):
         chunks = [CHUNKS[chunk] for chunk in tail]
         low, size = chunks[0][0], sum(size for _, size in chunks)
         parts = [part for chunk in tail for part in received[chunk]]
+        after = [] if index < 2 else [ticks[index - 2]]
         middle = pl.pallas_call(
             functools.partial(middle_kernel, chunks, count - 1),
             out_shape=jax.ShapeDtypeStruct((blocks * size, inner), bf16),
-            in_specs=[vmem] * (2 + len(parts)),
+            in_specs=[vmem] * (2 + len(parts)) + [anywhere] * len(after),
             out_specs=vmem,
             compiler_params=params,
             cost_estimate=cost(f"middle{index}"),
             name="middle",
-        )(own, gain_mid, *parts)
+        )(own, gain_mid, *parts, *after)
         other = lax.ppermute(middle, "strand", ring_pairs("strand", 1))
         operands = [middle, other, res, point] + ([] if out is None else [out])
-        out = pl.pallas_call(
-            functools.partial(final_kernel, low, size),
+        out, tick = pl.pallas_call(
+            functools.partial(final_kernel, low, size, len(operands)),
             grid=(1,),
-            out_shape=jax.ShapeDtypeStruct((blocks, DILATION, half), bf16),
+            out_shape=[
+                jax.ShapeDtypeStruct((blocks, DILATION, half), bf16),
+                jax.ShapeDtypeStruct((8, 128), f32),
+            ],
             in_specs=[vmem] * 4 + [anywhere] * (len(operands) - 4),
-            out_specs=pl.BlockSpec((blocks, size, half), lambda i, at=low // size: (0, at, 0)),
+            out_specs=[
+                pl.BlockSpec((blocks, size, half), lambda i, at=low // size: (0, at, 0)),
+                vmem,
+            ],
             input_output_aliases={} if out is None else {4: 0},
             compiler_params=params,
             cost_estimate=cost(f"final{index}"),
             name="final",
         )(*operands)
+        ticks.append(tick)
     return out.reshape(1, row_count, half)
 
 

time: 33.9 us -> 33.8 us (level)
  the two profiles are of different devices: /device:TPU:9 before, /device:TPU:17 now
where the time goes in v4:
time: 33.8 us; the launch traced here: 33.7 us
  Pallas kernels  16.4 us (49%)
  starting transfers between devices  13.8 us (41%)
  waiting for transfers between devices  3.39 us (10%)
    pallas_call x3, Pallas kernels, per_device(): pl.pallas_call(functools.partial(chunk_kernel, step, low, size, row_count...  5.11 us
    ppermute x3, starting transfers between devices, per_device(): other = lax.ppermute(middle, 'strand', ring_pairs('strand', 1))  4.87 us
    pallas_call x1, Pallas kernels, per_device(): pl.pallas_call(functools.partial(own_kernel, places, piece_rows), out_sha...  4.41 us
    pallas_call x3, Pallas kernels, per_device(): pl.pallas_call(functools.partial(final_kernel, low, size, len(operands)),...  3.26 us
    ppermute x3, starting transfers between devices, per_device(): received[index].append(lax.ppermute(part, 'dp', ring_pairs('dp', step)))  2.81 us
    ppermute x1, starting transfers between devices, per_device(): odd = lax.ppermute(joined, 'seq', pair_pairs('seq', 1))  1.91 us
    pallas_call x1, Pallas kernels, per_device(): pl.pallas_call(load_kernel, out_shape=jax.ShapeDtypeStruct((pack_rows, in...  1.7 us
    ppermute x1, waiting for transfers between devices, per_device(): piece = lax.ppermute(piece, 'groups', ring_pairs('groups', -turn))  1.66 us
  transfers between devices with their start and end apart: 11, of which 4 were waited for; matrix products, arithmetic and copies ran while one was open for 0% of the time, Pallas kernels for 46%

profile of v4, /device:TPU:17, one launch (start us, length us, event | category | flops | bytes accessed | tf_op | source)
XLA Modules:
  0.0 33.7 jit_solution(11916375691679027120)
XLA Ops:
  0.0 1.2 %collective-permute-start = (s32[1,512]{1,0:T(1,128)}, s32[1,512]{1,0:T(1,128)S(1)}, u32[]{:S(2)}, u32[]{:S(2)}) collective-permute-start(s32[1,512]{1,0:T(1,128)} %tok_any.1), channel_id=1, source_target_pairs={{0,2},{2,0},{1,3},{3,1},{4,6},{6,4},{5,7},{7,5},{8,10},{10,8},{9,1... | collective-permute-start | bytes 6152 | tf_op jit(solution)/shard_map/ppermute | solution.py:293
  1.2 1.0 %point_slice.1 = (bf16[192,768]{1,0:T(8,128)(2,1)S(1)}, s32[1,512]{1,0:T(1,128)S(1)}) custom-call(bf16[384,1536]{1,0:T(8,128)(2,1)} %refs_6_.1, s32[1,512]{1,0:T(1,128)} %tok_any.1), custom_call_target="tpu_custom_call" | custom-call | flops 100000000 | bytes 1048576 | tf_op jit(solution)/shard_map/point_slice/pallas_call | solution.py:295
  2.2 0.3 collective-permute-start.3
  2.7 1.4 %collective-permute-start.1 = (s32[1,1024]{1,0:T(1,128)S(1)}, s32[1,1024]{1,0:T(1,128)S(1)}, u32[]{:S(2)}, u32[]{:S(2)}) collective-permute-start(s32[1,1024]{1,0:T(1,128)S(1)} %join.1.refs_1_), channel_id=1, source_target_pairs={{0,4},{8,12},{4,0},{12,8},{1,5},{9,13},{5,1},{13,9},{2,6},{10,14},... | collective-permute-start | bytes 12296 | tf_op jit(solution)/shard_map/ppermute | solution.py:317
  4.0 1.9 %collective-permute-start.2 = (s32[1,1024]{1,0:T(1,128)S(1)}, s32[1,1024]{1,0:T(1,128)S(1)}, u32[]{:S(2)}, u32[]{:S(2)}) collective-permute-start(s32[1,1024]{1,0:T(1,128)S(1)} %join.1.refs_1_), channel_id=1, source_target_pairs={{4,8},{8,4},{5,9},{9,5},{6,10},{10,6},{7,11},{11,7},{20,24},{24,20... | collective-permute-start | bytes 12296 | tf_op jit(solution)/shard_map/ppermute | solution.py:318
  5.9 1.7 %load.1.refs_4_ = bf16[2496,768]{1,0:T(8,128)(2,1)S(1)} custom-call(bf16[15,4,1536]{2,1,0:T(4,128)(2,1)} %stem_any.1, bf16[3,768,768]{2,1,0:T(8,128)(2,1)} %refs_5_.1), custom_call_target="tpu_custom_call" | custom-call | flops 100000000 | bytes 1048576 | tf_op jit(solution)/shard_map/load/pallas_call | solution.py:320
  7.7 1.0 %collective-permute-done.2.refs_2_ = s32[1,1024]{1,0:T(1,128)S(1)} collective-permute-done((s32[1,1024]{1,0:T(1,128)S(1)}, s32[1,1024]{1,0:T(1,128)S(1)}, u32[]{:S(2)}, u32[]{:S(2)}) %collective-permute-start.2) | collective-permute-done | bytes 4128 | tf_op jit(solution)/shard_map/ppermute | solution.py:318
  8.7 1.9 %conv_sent.3 = (bf16[192,768]{1,0:T(8,128)(2,1)S(1)}, bf16[2496,768]{1,0:T(8,128)(2,1)S(1)}) custom-call(s32[1,1024]{1,0:T(1,128)S(1)} %collective-permute-done.1.refs_0_, s32[1,1024]{1,0:T(1,128)S(1)} %join.1.refs_1_, s32[1,1024]{1,0:T(1,128)S(1)} %collective-permute-done.2.refs_2_, f32[1536]{0:T(1024)S(1)} %copy-done, ...), custom_call_target="tpu_custom_call", output_to_operand_aliasing={{1}: (4, {})} | custom-call | flops 15000000512 | bytes 1048576 | tf_op jit(solution)/shard_map/conv_sent/pallas_call | solution.py:358
  10.5 1.3 %collective-permute-start.6 = (bf16[192,768]{1,0:T(8,128)(2,1)S(1)}, bf16[192,768]{1,0:T(8,128)(2,1)S(1)}, u32[]{:S(2)}, u32[]{:S(2)}) collective-permute-start(bf16[192,768]{1,0:T(8,128)(2,1)S(1)} %get-tuple-element.21.refs_6_), channel_id=1, source_target_pairs={{0,2},{2,0},{1,3},{3,1},{4,6},{6,4},{5,7},{7,5},{8,10},{10,8},{9,1... | collective-permute-start | bytes 884744 | tf_op jit(solution)/shard_map/ppermute | solution.py:375
  11.8 1.8 %conv_sent.4 = (bf16[192,768]{1,0:T(8,128)(2,1)S(1)}, bf16[192,768]{1,0:T(8,128)(2,1)S(1)}) custom-call(s32[1,1024]{1,0:T(1,128)S(1)} %collective-permute-done.1.refs_0_, s32[1,1024]{1,0:T(1,128)S(1)} %join.1.refs_1_, s32[1,1024]{1,0:T(1,128)S(1)} %collective-permute-done.2.refs_2_, f32[1536]{0:T(1024)S(1)} %copy-done, ...), custom_call_target="tpu_custom_call", output_to_operand_aliasing={{1}: (5, {})} | custom-call | flops 500000000 | bytes 1048576 | tf_op jit(solution)/shard_map/conv_sent/pallas_call | solution.py:358
  13.6 1.3 %collective-permute-start.4 = (bf16[192,768]{1,0:T(8,128)(2,1)S(1)}, bf16[192,768]{1,0:T(8,128)(2,1)S(1)}, u32[]{:S(2)}, u32[]{:S(2)}) collective-permute-start(bf16[192,768]{1,0:T(8,128)(2,1)S(1)} %get-tuple-element.23.refs_7_), channel_id=1, source_target_pairs={{0,16},{16,0},{1,17},{17,1},{2,18},{18,2},{3,19},{19,3},{4,20},{20... | collective-permute-start | bytes 884744 | tf_op jit(solution)/shard_map/ppermute | solution.py:382
  15.2 1.4 %conv_sent.5.refs_5_ = bf16[128,768]{1,0:T(8,128)(2,1)S(1)} custom-call(s32[1,1024]{1,0:T(1,128)S(1)} %collective-permute-done.1.refs_0_, s32[1,1024]{1,0:T(1,128)S(1)} %join.1.refs_1_, s32[1,1024]{1,0:T(1,128)S(1)} %collective-permute-done.2.refs_2_, f32[1536]{0:T(1024)S(1)} %copy-done, bf16[2496,768]{1,0:T(8,128)(2,1)S(1)} %get-tuple-element.19.refs_4_, ...), custom_call_target="tpu_custom_call" | custom-call | flops 5000000000 | bytes 1048576 | tf_op jit(solution)/shard_map/conv_sent/pallas_call | solution.py:358
  16.6 1.3 %collective-permute-start.5 = (bf16[128,768]{1,0:T(8,128)(2,1)S(1)}, bf16[128,768]{1,0:T(8,128)(2,1)S(1)}, u32[]{:S(2)}, u32[]{:S(2)}) collective-permute-start(bf16[128,768]{1,0:T(8,128)(2,1)S(1)} %conv_sent.5.refs_5_), channel_id=1, source_target_pairs={{0,2},{2,0},{1,3},{3,1},{4,6},{6,4},{5,7},{7,5},{8,10},{10,8},{9,1... | collective-permute-start | bytes 589832 | tf_op jit(solution)/shard_map/ppermute | solution.py:375
  17.9 1.7 %collective-permute-done.4.refs_8_ = bf16[192,768]{1,0:T(8,128)(2,1)S(1)} collective-permute-done((bf16[192,768]{1,0:T(8,128)(2,1)S(1)}, bf16[192,768]{1,0:T(8,128)(2,1)S(1)}, u32[]{:S(2)}, u32[]{:S(2)}) %collective-permute-start.4) | collective-permute-done | bytes 294944 | tf_op jit(solution)/shard_map/ppermute | solution.py:382
  19.6 4.4 %conv_own.1 = (f32[512,768]{1,0:T(8,128)S(1)}, f32[512,768]{1,0:T(8,128)S(1)}, bf16[768,768]{1,0:T(8,128)(2,1)S(1)}) custom-call(s32[1,1024]{1,0:T(1,128)S(1)} %collective-permute-done.1.refs_0_, s32[1,1024]{1,0:T(1,128)S(1)} %join.1.refs_1_, s32[1,1024]{1,0:T(1,128)S(1)} %collective-permute-done.2.refs_2_, f32[1536]{0:T(1024)S(1)} %copy-done, ...), custom_call_target="tpu_custom_call" | custom-call | flops 15000000512 | bytes 1048576 | tf_op jit(solution)/shard_map/conv_own/pallas_call | solution.py:386
  24.0 0.3 middle.3.mine_ref
  24.3 4.1 %collective-permute-start.7 = (bf16[192,768]{1,0:T(8,128)(2,1)S(1)}, bf16[192,768]{1,0:T(8,128)(2,1)S(1)}, u32[]{:S(2)}, u32[]{:S(2)}) collective-permute-start(bf16[192,768]{1,0:T(8,128)(2,1)S(1)} %middle.3.mine_ref), channel_id=1, source_target_pairs={{0,1},{1,0},{2,3},{3,2},{4,5},{5,4},{6,7},{7,6},{8,9},{9,8},{10,11... | collective-permute-start | bytes 884744 | tf_op jit(solution)/shard_map/ppermute | solution.py:420
  28.5 0.3 middle.5.mine_ref
  28.8 0.3 collective-permute-start.10
  29.1 0.6 %collective-permute-done.7.other_ref = bf16[192,768]{1,0:T(8,128)(2,1)S(1)} collective-permute-done((bf16[192,768]{1,0:T(8,128)(2,1)S(1)}, bf16[192,768]{1,0:T(8,128)(2,1)S(1)}, u32[]{:S(2)}, u32[]{:S(2)}) %collective-permute-start.7) | collective-permute-done | bytes 294944 | tf_op jit(solution)/shard_map/ppermute | solution.py:420
  29.7 1.1 %final.3 = (bf16[2,256,768]{2,1,0:T(8,128)(2,1)}, f32[8,128]{1,0:T(8,128)S(1)}) custom-call(bf16[192,768]{1,0:T(8,128)(2,1)S(1)} %middle.3.mine_ref, bf16[192,768]{1,0:T(8,128)(2,1)S(1)} %collective-permute-done.7.other_ref, f32[512,768]{1,0:T(8,128)S(1)} %get-tuple-element.25.res_ref, bf16[768,768]{1,0:T(8,128)(2,1)S(1)} %get-tuple-element.26.point_ref), custom_call_target="tpu_custom_call" | custom-call | flops 50000000 | bytes 1048576 | tf_op jit(solution)/shard_map/final/pallas_call | solution.py:422
  31.1 0.4 %collective-permute-start.8 = (bf16[128,768]{1,0:T(8,128)(2,1)S(1)}, bf16[128,768]{1,0:T(8,128)(2,1)S(1)}, u32[]{:S(2)}, u32[]{:S(2)}) collective-permute-start(bf16[128,768]{1,0:T(8,128)(2,1)S(1)} %middle.4.mine_ref), channel_id=1, source_target_pairs={{0,1},{1,0},{2,3},{3,2},{4,5},{5,4},{6,7},{7,6},{8,9},{9,8},{10,11... | collective-permute-start | bytes 589832 | tf_op jit(solution)/shard_map/ppermute | solution.py:420
  31.5 1.1 %final.4 = (bf16[2,256,768]{2,1,0:T(8,128)(2,1)}, f32[8,128]{1,0:T(8,128)}) custom-call(bf16[192,768]{1,0:T(8,128)(2,1)S(1)} %middle.5.mine_ref, bf16[192,768]{1,0:T(8,128)(2,1)S(1)} %collective-permute-done.10.other_ref, f32[512,768]{1,0:T(8,128)S(1)} %get-tuple-element.25.res_ref, ...), custom_call_target="tpu_custom_call", output_to_operand_aliasing={{0}: (4, {})} | custom-call | flops 500000000 | bytes 1048576 | tf_op jit(solution)/shard_map/final/pallas_call | solution.py:422
  32.6 1.0 %final.5 = (bf16[2,256,768]{2,1,0:T(8,128)(2,1)}, f32[8,128]{1,0:T(8,128)}) custom-call(bf16[128,768]{1,0:T(8,128)(2,1)S(1)} %middle.4.mine_ref, bf16[128,768]{1,0:T(8,128)(2,1)S(1)} %collective-permute-done.8.other_ref, f32[512,768]{1,0:T(8,128)S(1)} %get-tuple-element.25.res_ref, ...), custom_call_target="tpu_custom_call", output_to_operand_aliasing={{0}: (4, {})} | custom-call | flops 15000000512 | bytes 1048576 | tf_op jit(solution)/shard_map/final/pallas_call | solution.py:422
  (15 shorter events, 0.7 us)
Async XLA Ops:
  0.0 2.6 %collective-permute-start = (s32[1,512]{1,0:T(1,128)}, s32[1,512]{1,0:T(1,128)S(1)}, u32[]{:S(2)}, u32[]{:S(2)}) collective-permute-start(s32[1,512]{1,0:T(1,128)} %tok_any.1), channel_id=1, source_target_pairs={{0,2},{2,0},{1,3},{3,1},{4,6},{6,4},{5,7},{7,5},{8,10},{10,8},{9,1... | collective-permute-start | bytes 6152 | tf_op jit(solution)/shard_map/ppermute | solution.py:293
  2.2 9.6 %collective-permute-start.3 = (bf16[192,768]{1,0:T(8,128)(2,1)S(1)}, bf16[192,768]{1,0:T(8,128)(2,1)S(1)}, u32[]{:S(2)}, u32[]{:S(2)}) collective-permute-start(bf16[192,768]{1,0:T(8,128)(2,1)S(1)} %get-tuple-element.20), channel_id=1, source_target_pairs={{0,2},{2,0},{1,3},{3,1},{4,6},{6,4},{5,7},{7,5},{8,10},{10,8},{9,1... | collective-permute-start | bytes 884744 | tf_op jit(solution)/shard_map/ppermute | solution.py:335
  2.7 6.0 %copy-start = (f32[1536]{0:T(1024)S(1)}, f32[1536]{0:T(1024)}, u32[]{:S(2)}) copy-start(f32[1536]{0:T(1024)} %refs_3_.7) | copy-start | bytes 18436
  2.7 5.0 %collective-permute-start.1 = (s32[1,1024]{1,0:T(1,128)S(1)}, s32[1,1024]{1,0:T(1,128)S(1)}, u32[]{:S(2)}, u32[]{:S(2)}) collective-permute-start(s32[1,1024]{1,0:T(1,128)S(1)} %join.1.refs_1_), channel_id=1, source_target_pairs={{0,4},{8,12},{4,0},{12,8},{1,5},{9,13},{5,1},{13,9},{2,6},{10,14},... | collective-permute-start | bytes 12296 | tf_op jit(solution)/shard_map/ppermute | solution.py:317
  4.0 4.6 %collective-permute-start.2 = (s32[1,1024]{1,0:T(1,128)S(1)}, s32[1,1024]{1,0:T(1,128)S(1)}, u32[]{:S(2)}, u32[]{:S(2)}) collective-permute-start(s32[1,1024]{1,0:T(1,128)S(1)} %join.1.refs_1_), channel_id=1, source_target_pairs={{4,8},{8,4},{5,9},{9,5},{6,10},{10,6},{7,11},{11,7},{20,24},{24,20... | collective-permute-start | bytes 12296 | tf_op jit(solution)/shard_map/ppermute | solution.py:318
  10.5 13.5 %collective-permute-start.6 = (bf16[192,768]{1,0:T(8,128)(2,1)S(1)}, bf16[192,768]{1,0:T(8,128)(2,1)S(1)}, u32[]{:S(2)}, u32[]{:S(2)}) collective-permute-start(bf16[192,768]{1,0:T(8,128)(2,1)S(1)} %get-tuple-element.21.refs_6_), channel_id=1, source_target_pairs={{0,2},{2,0},{1,3},{3,1},{4,6},{6,4},{5,7},{7,5},{8,10},{10,8},{9,1... | collective-permute-start | bytes 884744 | tf_op jit(solution)/shard_map/ppermute | solution.py:375
  13.6 5.9 %collective-permute-start.4 = (bf16[192,768]{1,0:T(8,128)(2,1)S(1)}, bf16[192,768]{1,0:T(8,128)(2,1)S(1)}, u32[]{:S(2)}, u32[]{:S(2)}) collective-permute-start(bf16[192,768]{1,0:T(8,128)(2,1)S(1)} %get-tuple-element.23.refs_7_), channel_id=1, source_target_pairs={{0,16},{16,0},{1,17},{17,1},{2,18},{18,2},{3,19},{19,3},{4,20},{20... | collective-permute-start | bytes 884744 | tf_op jit(solution)/shard_map/ppermute | solution.py:382
  15.0 13.5 %collective-permute-start.9 = (bf16[192,768]{1,0:T(8,128)(2,1)S(1)}, bf16[192,768]{1,0:T(8,128)(2,1)S(1)}, u32[]{:S(2)}, u32[]{:S(2)}) collective-permute-start(bf16[192,768]{1,0:T(8,128)(2,1)S(1)} %get-tuple-element.22.refs_5_), channel_id=1, source_target_pairs={{0,2},{2,0},{1,3},{3,1},{4,6},{6,4},{5,7},{7,5},{8,10},{10,8},{9,1... | collective-permute-start | bytes 884744 | tf_op jit(solution)/shard_map/ppermute | solution.py:375
  16.6 7.4 %copy-start.1 = (f32[768]{0:T(1024)S(1)}, f32[768]{0:T(1024)}, u32[]{:S(2)}) copy-start(f32[768]{0:T(1024)} %gain_ref.5) | copy-start | bytes 9220
  16.6 14.2 %collective-permute-start.5 = (bf16[128,768]{1,0:T(8,128)(2,1)S(1)}, bf16[128,768]{1,0:T(8,128)(2,1)S(1)}, u32[]{:S(2)}, u32[]{:S(2)}) collective-permute-start(bf16[128,768]{1,0:T(8,128)(2,1)S(1)} %conv_sent.5.refs_5_), channel_id=1, source_target_pairs={{0,2},{2,0},{1,3},{3,1},{4,6},{6,4},{5,7},{7,5},{8,10},{10,8},{9,1... | collective-permute-start | bytes 589832 | tf_op jit(solution)/shard_map/ppermute | solution.py:375
  24.3 5.3 %collective-permute-start.7 = (bf16[192,768]{1,0:T(8,128)(2,1)S(1)}, bf16[192,768]{1,0:T(8,128)(2,1)S(1)}, u32[]{:S(2)}, u32[]{:S(2)}) collective-permute-start(bf16[192,768]{1,0:T(8,128)(2,1)S(1)} %middle.3.mine_ref), channel_id=1, source_target_pairs={{0,1},{1,0},{2,3},{3,2},{4,5},{5,4},{6,7},{7,6},{8,9},{9,8},{10,11... | collective-permute-start | bytes 884744 | tf_op jit(solution)/shard_map/ppermute | solution.py:420
  28.8 2.7 %collective-permute-start.10 = (bf16[192,768]{1,0:T(8,128)(2,1)S(1)}, bf16[192,768]{1,0:T(8,128)(2,1)S(1)}, u32[]{:S(2)}, u32[]{:S(2)}) collective-permute-start(bf16[192,768]{1,0:T(8,128)(2,1)S(1)} %middle.5.mine_ref), channel_id=1, source_target_pairs={{0,1},{1,0},{2,3},{3,2},{4,5},{5,4},{6,7},{7,6},{8,9},{9,8},{10,11... | collective-permute-start | bytes 884744 | tf_op jit(solution)/shard_map/ppermute | solution.py:420
  31.1 1.6 %collective-permute-start.8 = (bf16[128,768]{1,0:T(8,128)(2,1)S(1)}, bf16[128,768]{1,0:T(8,128)(2,1)S(1)}, u32[]{:S(2)}, u32[]{:S(2)}) collective-permute-start(bf16[128,768]{1,0:T(8,128)(2,1)S(1)} %middle.4.mine_ref), channel_id=1, source_target_pairs={{0,1},{1,0},{2,3},{3,2},{4,5},{5,4},{6,7},{7,6},{8,9},{9,8},{10,11... | collective-permute-start | bytes 589832 | tf_op jit(solution)/shard_map/ppermute | solution.py:420

commit v5 on v4

--- a/solution.py
+++ b/solution.py
@@ -12,7 +12,7 @@
 ROW_STEP = 32
 CHUNKS = ((0, 96), (96, 96), (192, 64))
 TAILS = ((0,), (1,), (2,))
-EARLY_TAPS, LATE_TAPS = (0, 1), (2,)
+EARLY_TAPS, LATE_TAPS = (0, 1, 2), ()
 KINDS = 4
 TABLE = 16 * KINDS
 WEIGHTS = {
@@ -338,7 +338,8 @@
     for step in range(1, count):
         for index, (low, size) in enumerate(CHUNKS):
             rows = row_count // DILATION * size
-            loading, passing = step == 1 and index == 0, index == 1
+            loading = bool(LATE_TAPS) and step == 1 and index == 0
+            passing = index == 1
             operands = [even, joined, odd, gain_in, pack]
             shapes = [jax.ShapeDtypeStruct((rows, inner), bf16)]
             scratch = [pltpu.VMEM((rows + 2 * size, depth), bf16)]

time: 33.8 us -> 33.8 us (level)
  the two profiles are of different devices: /device:TPU:17 before, /device:TPU:13 now
where the time goes in v5:
time: 33.8 us; the launch traced here: 33.7 us
  Pallas kernels  16.6 us (49%)
  starting transfers between devices  13.8 us (41%)
  waiting for transfers between devices  3.11 us (9%)
    pallas_call x3, Pallas kernels, per_device(): pl.pallas_call(functools.partial(chunk_kernel, step, low, size, row_count...  5.01 us
    ppermute x3, starting transfers between devices, per_device(): other = lax.ppermute(middle, 'strand', ring_pairs('strand', 1))  4.63 us
    pallas_call x1, Pallas kernels, per_device(): pl.pallas_call(functools.partial(own_kernel, places, piece_rows), out_sha...  4.41 us
    ppermute x1, starting transfers between devices, per_device(): odd = lax.ppermute(joined, 'seq', pair_pairs('seq', 1))  4.32 us
    pallas_call x3, Pallas kernels, per_device(): pl.pallas_call(functools.partial(final_kernel, low, size, len(operands)),...  3.26 us
    ppermute x3, starting transfers between devices, per_device(): received[index].append(lax.ppermute(part, 'dp', ring_pairs('dp', step)))  2.8 us
    ppermute x1, waiting for transfers between devices, per_device(): piece = lax.ppermute(piece, 'groups', ring_pairs('groups', -turn))  2.68 us
    pallas_call x1, Pallas kernels, per_device(): pl.pallas_call(load_kernel, out_shape=jax.ShapeDtypeStruct((pack_rows, in...  2.07 us
  transfers between devices with their start and end apart: 11, of which 3 were waited for; matrix products, arithmetic and copies ran while one was open for 0% of the time, Pallas kernels for 46%

profile of v5, /device:TPU:13, one launch (start us, length us, event | category | flops | bytes accessed | tf_op | source)
XLA Modules:
  0.0 33.7 jit_solution(6360205777732034347)
XLA Ops:
  0.0 1.2 %collective-permute-start = (s32[1,512]{1,0:T(1,128)}, s32[1,512]{1,0:T(1,128)S(1)}, u32[]{:S(2)}, u32[]{:S(2)}) collective-permute-start(s32[1,512]{1,0:T(1,128)} %tok_any.1), channel_id=1, source_target_pairs={{0,2},{2,0},{1,3},{3,1},{4,6},{6,4},{5,7},{7,5},{8,10},{10,8},{9,1... | collective-permute-start | bytes 6152 | tf_op jit(solution)/shard_map/ppermute | solution.py:293
  1.2 1.0 %point_slice.1 = (bf16[192,768]{1,0:T(8,128)(2,1)S(1)}, s32[1,512]{1,0:T(1,128)S(1)}) custom-call(bf16[384,1536]{1,0:T(8,128)(2,1)} %refs_6_.1, s32[1,512]{1,0:T(1,128)} %tok_any.1), custom_call_target="tpu_custom_call" | custom-call | flops 100000000 | bytes 1048576 | tf_op jit(solution)/shard_map/point_slice/pallas_call | solution.py:295
  2.2 0.3 collective-permute-start.3
  2.9 4.3 %collective-permute-start.2 = (s32[1,1024]{1,0:T(1,128)S(1)}, s32[1,1024]{1,0:T(1,128)S(1)}, u32[]{:S(2)}, u32[]{:S(2)}) collective-permute-start(s32[1,1024]{1,0:T(1,128)S(1)} %join.1.refs_1_), channel_id=1, source_target_pairs={{4,8},{8,4},{5,9},{9,5},{6,10},{10,6},{7,11},{11,7},{20,24},{24,20... | collective-permute-start | bytes 12296 | tf_op jit(solution)/shard_map/ppermute | solution.py:318
  7.2 2.1 %load.1.refs_4_ = bf16[2496,768]{1,0:T(8,128)(2,1)S(1)} custom-call(bf16[15,4,1536]{2,1,0:T(4,128)(2,1)} %stem_any.1, bf16[3,768,768]{2,1,0:T(8,128)(2,1)} %w_any.1), custom_call_target="tpu_custom_call" | custom-call | flops 100000000 | bytes 1048576 | tf_op jit(solution)/shard_map/load/pallas_call | solution.py:320
  9.3 1.8 %conv_sent.3.refs_6_ = bf16[192,768]{1,0:T(8,128)(2,1)S(1)} custom-call(s32[1,1024]{1,0:T(1,128)S(1)} %collective-permute-done.1.refs_0_, s32[1,1024]{1,0:T(1,128)S(1)} %join.1.refs_1_, s32[1,1024]{1,0:T(1,128)S(1)} %collective-permute-done.2.refs_2_, f32[1536]{0:T(1024)S(1)} %copy-done, bf16[2496,768]{1,0:T(8,128)(2,1)S(1)} %load.1.refs_4_), custom_call_target="tpu_custom_call" | custom-call | flops 15000000512 | bytes 1048576 | tf_op jit(solution)/shard_map/conv_sent/pallas_call | solution.py:359
  11.1 1.3 %collective-permute-start.6 = (bf16[192,768]{1,0:T(8,128)(2,1)S(1)}, bf16[192,768]{1,0:T(8,128)(2,1)S(1)}, u32[]{:S(2)}, u32[]{:S(2)}) collective-permute-start(bf16[192,768]{1,0:T(8,128)(2,1)S(1)} %conv_sent.3.refs_6_), channel_id=1, source_target_pairs={{0,2},{2,0},{1,3},{3,1},{4,6},{6,4},{5,7},{7,5},{8,10},{10,8},{9,1... | collective-permute-start | bytes 884744 | tf_op jit(solution)/shard_map/ppermute | solution.py:376
  12.4 1.8 %conv_sent.4 = (bf16[192,768]{1,0:T(8,128)(2,1)S(1)}, bf16[192,768]{1,0:T(8,128)(2,1)S(1)}) custom-call(s32[1,1024]{1,0:T(1,128)S(1)} %collective-permute-done.1.refs_0_, s32[1,1024]{1,0:T(1,128)S(1)} %join.1.refs_1_, s32[1,1024]{1,0:T(1,128)S(1)} %collective-permute-done.2.refs_2_, f32[1536]{0:T(1024)S(1)} %copy-done, ...), custom_call_target="tpu_custom_call", output_to_operand_aliasing={{1}: (5, {})} | custom-call | flops 500000000 | bytes 1048576 | tf_op jit(solution)/shard_map/conv_sent/pallas_call | solution.py:359
  14.2 0.3 collective-permute-start.4
  14.5 0.3 collective-permute-start.9
  14.8 1.4 %conv_sent.5.refs_5_ = bf16[128,768]{1,0:T(8,128)(2,1)S(1)} custom-call(s32[1,1024]{1,0:T(1,128)S(1)} %collective-permute-done.1.refs_0_, s32[1,1024]{1,0:T(1,128)S(1)} %join.1.refs_1_, s32[1,1024]{1,0:T(1,128)S(1)} %collective-permute-done.2.refs_2_, f32[1536]{0:T(1024)S(1)} %copy-done, bf16[2496,768]{1,0:T(8,128)(2,1)S(1)} %load.1.refs_4_, ...), custom_call_target="tpu_custom_call" | custom-call | flops 5000000000 | bytes 1048576 | tf_op jit(solution)/shard_map/conv_sent/pallas_call | solution.py:359
  16.2 1.3 %collective-permute-start.5 = (bf16[128,768]{1,0:T(8,128)(2,1)S(1)}, bf16[128,768]{1,0:T(8,128)(2,1)S(1)}, u32[]{:S(2)}, u32[]{:S(2)}) collective-permute-start(bf16[128,768]{1,0:T(8,128)(2,1)S(1)} %conv_sent.5.refs_5_), channel_id=1, source_target_pairs={{0,2},{2,0},{1,3},{3,1},{4,6},{6,4},{5,7},{7,5},{8,10},{10,8},{9,1... | collective-permute-start | bytes 589832 | tf_op jit(solution)/shard_map/ppermute | solution.py:376
  17.5 2.7 %collective-permute-done.4.refs_8_ = bf16[192,768]{1,0:T(8,128)(2,1)S(1)} collective-permute-done((bf16[192,768]{1,0:T(8,128)(2,1)S(1)}, bf16[192,768]{1,0:T(8,128)(2,1)S(1)}, u32[]{:S(2)}, u32[]{:S(2)}) %collective-permute-start.4) | collective-permute-done | bytes 294944 | tf_op jit(solution)/shard_map/ppermute | solution.py:383
  20.2 4.4 %conv_own.1 = (f32[512,768]{1,0:T(8,128)S(1)}, f32[512,768]{1,0:T(8,128)S(1)}, bf16[768,768]{1,0:T(8,128)(2,1)S(1)}) custom-call(s32[1,1024]{1,0:T(1,128)S(1)} %collective-permute-done.1.refs_0_, s32[1,1024]{1,0:T(1,128)S(1)} %join.1.refs_1_, s32[1,1024]{1,0:T(1,128)S(1)} %collective-permute-done.2.refs_2_, f32[1536]{0:T(1024)S(1)} %copy-done, ...), custom_call_target="tpu_custom_call" | custom-call | flops 15000000512 | bytes 1048576 | tf_op jit(solution)/shard_map/conv_own/pallas_call | solution.py:387
  24.6 0.3 middle.3.mine_ref
  24.9 3.6 %collective-permute-start.7 = (bf16[192,768]{1,0:T(8,128)(2,1)S(1)}, bf16[192,768]{1,0:T(8,128)(2,1)S(1)}, u32[]{:S(2)}, u32[]{:S(2)}) collective-permute-start(bf16[192,768]{1,0:T(8,128)(2,1)S(1)} %middle.3.mine_ref), channel_id=1, source_target_pairs={{0,1},{1,0},{2,3},{3,2},{4,5},{5,4},{6,7},{7,6},{8,9},{9,8},{10,11... | collective-permute-start | bytes 884744 | tf_op jit(solution)/shard_map/ppermute | solution.py:421
  28.5 0.3 middle.5.mine_ref
  28.8 0.6 %collective-permute-start.10 = (bf16[192,768]{1,0:T(8,128)(2,1)S(1)}, bf16[192,768]{1,0:T(8,128)(2,1)S(1)}, u32[]{:S(2)}, u32[]{:S(2)}) collective-permute-start(bf16[192,768]{1,0:T(8,128)(2,1)S(1)} %middle.5.mine_ref), channel_id=1, source_target_pairs={{0,1},{1,0},{2,3},{3,2},{4,5},{5,4},{6,7},{7,6},{8,9},{9,8},{10,11... | collective-permute-start | bytes 884744 | tf_op jit(solution)/shard_map/ppermute | solution.py:421
  29.4 0.3 collective-permute-done.7.other_ref
  29.7 1.1 %final.3 = (bf16[2,256,768]{2,1,0:T(8,128)(2,1)}, f32[8,128]{1,0:T(8,128)S(1)}) custom-call(bf16[192,768]{1,0:T(8,128)(2,1)S(1)} %middle.3.mine_ref, bf16[192,768]{1,0:T(8,128)(2,1)S(1)} %collective-permute-done.7.other_ref, f32[512,768]{1,0:T(8,128)S(1)} %get-tuple-element.21.res_ref, bf16[768,768]{1,0:T(8,128)(2,1)S(1)} %get-tuple-element.22.point_ref), custom_call_target="tpu_custom_call" | custom-call | flops 50000000 | bytes 1048576 | tf_op jit(solution)/shard_map/final/pallas_call | solution.py:423
  30.8 0.3 middle.4.mine_ref
  31.1 0.4 %collective-permute-start.8 = (bf16[128,768]{1,0:T(8,128)(2,1)S(1)}, bf16[128,768]{1,0:T(8,128)(2,1)S(1)}, u32[]{:S(2)}, u32[]{:S(2)}) collective-permute-start(bf16[128,768]{1,0:T(8,128)(2,1)S(1)} %middle.4.mine_ref), channel_id=1, source_target_pairs={{0,1},{1,0},{2,3},{3,2},{4,5},{5,4},{6,7},{7,6},{8,9},{9,8},{10,11... | collective-permute-start | bytes 589832 | tf_op jit(solution)/shard_map/ppermute | solution.py:421
  31.5 1.1 %final.4 = (bf16[2,256,768]{2,1,0:T(8,128)(2,1)}, f32[8,128]{1,0:T(8,128)}) custom-call(bf16[192,768]{1,0:T(8,128)(2,1)S(1)} %middle.5.mine_ref, bf16[192,768]{1,0:T(8,128)(2,1)S(1)} %collective-permute-done.10.other_ref, f32[512,768]{1,0:T(8,128)S(1)} %get-tuple-element.21.res_ref, ...), custom_call_target="tpu_custom_call", output_to_operand_aliasing={{0}: (4, {})} | custom-call | flops 500000000 | bytes 1048576 | tf_op jit(solution)/shard_map/final/pallas_call | solution.py:423
  32.7 1.0 %final.5 = (bf16[2,256,768]{2,1,0:T(8,128)(2,1)}, f32[8,128]{1,0:T(8,128)}) custom-call(bf16[128,768]{1,0:T(8,128)(2,1)S(1)} %middle.4.mine_ref, bf16[128,768]{1,0:T(8,128)(2,1)S(1)} %collective-permute-done.8.other_ref, f32[512,768]{1,0:T(8,128)S(1)} %get-tuple-element.21.res_ref, ...), custom_call_target="tpu_custom_call", output_to_operand_aliasing={{0}: (4, {})} | custom-call | flops 15000000512 | bytes 1048576 | tf_op jit(solution)/shard_map/final/pallas_call | solution.py:423
  (15 shorter events, 0.4 us)
Async XLA Ops:
  0.0 2.6 %collective-permute-start = (s32[1,512]{1,0:T(1,128)}, s32[1,512]{1,0:T(1,128)S(1)}, u32[]{:S(2)}, u32[]{:S(2)}) collective-permute-start(s32[1,512]{1,0:T(1,128)} %tok_any.1), channel_id=1, source_target_pairs={{0,2},{2,0},{1,3},{3,1},{4,6},{6,4},{5,7},{7,5},{8,10},{10,8},{9,1... | collective-permute-start | bytes 6152 | tf_op jit(solution)/shard_map/ppermute | solution.py:293
  2.2 10.2 %collective-permute-start.3 = (bf16[192,768]{1,0:T(8,128)(2,1)S(1)}, bf16[192,768]{1,0:T(8,128)(2,1)S(1)}, u32[]{:S(2)}, u32[]{:S(2)}) collective-permute-start(bf16[192,768]{1,0:T(8,128)(2,1)S(1)} %get-tuple-element.17), channel_id=1, source_target_pairs={{0,2},{2,0},{1,3},{3,1},{4,6},{6,4},{5,7},{7,5},{8,10},{10,8},{9,1... | collective-permute-start | bytes 884744 | tf_op jit(solution)/shard_map/ppermute | solution.py:335
  2.7 6.7 %copy-start = (f32[1536]{0:T(1024)S(1)}, f32[1536]{0:T(1024)}, u32[]{:S(2)}) copy-start(f32[1536]{0:T(1024)} %refs_3_.7) | copy-start | bytes 18436
  2.7 6.6 %collective-permute-start.1 = (s32[1,1024]{1,0:T(1,128)S(1)}, s32[1,1024]{1,0:T(1,128)S(1)}, u32[]{:S(2)}, u32[]{:S(2)}) collective-permute-start(s32[1,1024]{1,0:T(1,128)S(1)} %join.1.refs_1_), channel_id=1, source_target_pairs={{0,4},{8,12},{4,0},{12,8},{1,5},{9,13},{5,1},{13,9},{2,6},{10,14},... | collective-permute-start | bytes 12296 | tf_op jit(solution)/shard_map/ppermute | solution.py:317
  2.9 6.4 %collective-permute-start.2 = (s32[1,1024]{1,0:T(1,128)S(1)}, s32[1,1024]{1,0:T(1,128)S(1)}, u32[]{:S(2)}, u32[]{:S(2)}) collective-permute-start(s32[1,1024]{1,0:T(1,128)S(1)} %join.1.refs_1_), channel_id=1, source_target_pairs={{4,8},{8,4},{5,9},{9,5},{6,10},{10,6},{7,11},{11,7},{20,24},{24,20... | collective-permute-start | bytes 12296 | tf_op jit(solution)/shard_map/ppermute | solution.py:318
  11.1 13.4 %collective-permute-start.6 = (bf16[192,768]{1,0:T(8,128)(2,1)S(1)}, bf16[192,768]{1,0:T(8,128)(2,1)S(1)}, u32[]{:S(2)}, u32[]{:S(2)}) collective-permute-start(bf16[192,768]{1,0:T(8,128)(2,1)S(1)} %conv_sent.3.refs_6_), channel_id=1, source_target_pairs={{0,2},{2,0},{1,3},{3,1},{4,6},{6,4},{5,7},{7,5},{8,10},{10,8},{9,1... | collective-permute-start | bytes 884744 | tf_op jit(solution)/shard_map/ppermute | solution.py:376
  14.2 5.9 %collective-permute-start.4 = (bf16[192,768]{1,0:T(8,128)(2,1)S(1)}, bf16[192,768]{1,0:T(8,128)(2,1)S(1)}, u32[]{:S(2)}, u32[]{:S(2)}) collective-permute-start(bf16[192,768]{1,0:T(8,128)(2,1)S(1)} %get-tuple-element.19.refs_7_), channel_id=1, source_target_pairs={{0,16},{16,0},{1,17},{17,1},{2,18},{18,2},{3,19},{19,3},{4,20},{20... | collective-permute-start | bytes 884744 | tf_op jit(solution)/shard_map/ppermute | solution.py:383
  14.5 14.0 %collective-permute-start.9 = (bf16[192,768]{1,0:T(8,128)(2,1)S(1)}, bf16[192,768]{1,0:T(8,128)(2,1)S(1)}, u32[]{:S(2)}, u32[]{:S(2)}) collective-permute-start(bf16[192,768]{1,0:T(8,128)(2,1)S(1)} %get-tuple-element.18.refs_5_), channel_id=1, source_target_pairs={{0,2},{2,0},{1,3},{3,1},{4,6},{6,4},{5,7},{7,5},{8,10},{10,8},{9,1... | collective-permute-start | bytes 884744 | tf_op jit(solution)/shard_map/ppermute | solution.py:376
  16.2 8.4 %copy-start.1 = (f32[768]{0:T(1024)S(1)}, f32[768]{0:T(1024)}, u32[]{:S(2)}) copy-start(f32[768]{0:T(1024)} %gain_ref.5) | copy-start | bytes 9220
  16.2 14.6 %collective-permute-start.5 = (bf16[128,768]{1,0:T(8,128)(2,1)S(1)}, bf16[128,768]{1,0:T(8,128)(2,1)S(1)}, u32[]{:S(2)}, u32[]{:S(2)}) collective-permute-start(bf16[128,768]{1,0:T(8,128)(2,1)S(1)} %conv_sent.5.refs_5_), channel_id=1, source_target_pairs={{0,2},{2,0},{1,3},{3,1},{4,6},{6,4},{5,7},{7,5},{8,10},{10,8},{9,1... | collective-permute-start | bytes 589832 | tf_op jit(solution)/shard_map/ppermute | solution.py:376
  24.9 4.8 %collective-permute-start.7 = (bf16[192,768]{1,0:T(8,128)(2,1)S(1)}, bf16[192,768]{1,0:T(8,128)(2,1)S(1)}, u32[]{:S(2)}, u32[]{:S(2)}) collective-permute-start(bf16[192,768]{1,0:T(8,128)(2,1)S(1)} %middle.3.mine_ref), channel_id=1, source_target_pairs={{0,1},{1,0},{2,3},{3,2},{4,5},{5,4},{6,7},{7,6},{8,9},{9,8},{10,11... | collective-permute-start | bytes 884744 | tf_op jit(solution)/shard_map/ppermute | solution.py:421
  28.8 2.7 %collective-permute-start.10 = (bf16[192,768]{1,0:T(8,128)(2,1)S(1)}, bf16[192,768]{1,0:T(8,128)(2,1)S(1)}, u32[]{:S(2)}, u32[]{:S(2)}) collective-permute-start(bf16[192,768]{1,0:T(8,128)(2,1)S(1)} %middle.5.mine_ref), channel_id=1, source_target_pairs={{0,1},{1,0},{2,3},{3,2},{4,5},{5,4},{6,7},{7,6},{8,9},{9,8},{10,11... | collective-permute-start | bytes 884744 | tf_op jit(solution)/shard_map/ppermute | solution.py:421
  31.1 1.6 %collective-permute-start.8 = (bf16[128,768]{1,0:T(8,128)(2,1)S(1)}, bf16[128,768]{1,0:T(8,128)(2,1)S(1)}, u32[]{:S(2)}, u32[]{:S(2)}) collective-permute-start(bf16[128,768]{1,0:T(8,128)(2,1)S(1)} %middle.4.mine_ref), channel_id=1, source_target_pairs={{0,1},{1,0},{2,3},{3,2},{4,5},{5,4},{6,7},{7,6},{8,9},{9,8},{10,11... | collective-permute-start | bytes 589832 | tf_op jit(solution)/shard_map/ppermute | solution.py:421
